TPU v7x, 32 devices: a whole 2x2x4 slice. The times are simulated.
32 devices in a mesh: dp: 4 (over y, x), own: 8 (over z, core).
Axes of the slice: x: 2, y: 2, z: 4, core: 2. Of those that a mesh axis runs over, the one named last changes fastest.
Arguments:
- partial_grads: bfloat16 [4, 8, 512, 512], P('dp', None, 'own'), may hold values from -6 to 6
- owner_list: int32 [8], replicated, may hold values from 0 to 7, as said below
- left_stat: float32 [16, 512, 512], P('own', 'dp'), may hold values from -6 to 6
- right_stat: float32 [16, 512, 512], P('own', 'dp'), may hold values from -6 to 6
- left_root: bfloat16 [16, 512, 512], P('own', 'dp'), as said below
- right_root: bfloat16 [16, 512, 512], P('own', 'dp'), as said below
Outputs:
- new_left: float32 [16, 512, 512], P('own', 'dp')
- new_right: float32 [16, 512, 512], P('own', 'dp')
- update: bfloat16 [8, 512, 512], P(None, 'own', 'dp')
Inputs may be any that keep to these rules, and one draw needn't show every extreme that they name: `owner_list`: each owner is named by at most 2 blocks; a quarter of the owners are named by exactly 2 blocks, half by one, a quarter by none. `left_root`: each matrix is symmetric and positive definite. `right_root`: each matrix is symmetric and positive definite.
All inputs are finite; a program needn't handle non-finite values.
Results may differ from a plain program's by a relative error of at most 0.015.
Values may be sent and summed in bfloat16 or wider, within the bound.
A program may use at most 64 MiB of HBM per device.

v0:
```python
import jax
import jax.numpy as jnp
from jax import lax
from jax.sharding import PartitionSpec as P

decay_rate = 0.95
epsilon = 1e-06


def body(partial_grads, owner_list, left_stat, right_stat, left_root, right_root):
    owners = lax.axis_size("own")
    capacity = left_stat.shape[0]
    quarter = left_stat.shape[1]
    block_width = left_stat.shape[2]
    blocks = owner_list.shape[0]
    owner_hits = (owner_list[:, None] == jnp.arange(owners, dtype=jnp.int32)[None, :]).astype(
        jnp.int32
    )
    before = jnp.cumsum(owner_hits, axis=0) - owner_hits
    slot_index = jnp.sum(before * owner_hits, axis=1)
    slot_hits = (slot_index[:, None] == jnp.arange(capacity, dtype=jnp.int32)[None, :]).astype(
        jnp.int32
    )
    slot_match = slot_hits[:, :, None] * owner_hits[:, None, :]
    source_block = jnp.sum(slot_match * jnp.arange(blocks, dtype=jnp.int32)[:, None, None], axis=0)
    filled_flag = jnp.sum(slot_match, axis=0).astype(jnp.bfloat16)
    local_terms = partial_grads[0].astype(jnp.float32)
    shared = lax.psum(local_terms.astype(jnp.bfloat16), "dp")
    outgoing = jnp.take(shared, source_block, axis=0) * filled_flag[:, :, None, None]
    arrived = lax.all_to_all(outgoing, "own", split_axis=1, concat_axis=1, tiled=True)
    grad_part = arrived.reshape(capacity, block_width, arrived.shape[3])
    dp_lane = lax.axis_index("dp")
    own_index = lax.axis_index("own")
    owner_load = jnp.sum((owner_list == own_index).astype(jnp.int32))
    slot_used = (jnp.arange(capacity, dtype=jnp.int32) < owner_load)[:, None, None]
    row_start = dp_lane * quarter
    grad_rows = lax.dynamic_slice_in_dim(grad_part, row_start, quarter, 1)
    grad_colq = lax.dynamic_slice_in_dim(grad_part, row_start, quarter, 2)
    left_gram = jnp.einsum("cqk,cnk->cqn", grad_rows, grad_part, preferred_element_type=jnp.float32)
    right_gram = jnp.einsum(
        "ckq,ckn->cqn", grad_colq, grad_part, preferred_element_type=jnp.float32
    )
    new_left = jnp.where(slot_used, decay_rate * left_stat + left_gram / block_width, left_stat)
    new_right = jnp.where(slot_used, decay_rate * right_stat + right_gram / block_width, right_stat)
    half_done = jnp.einsum(
        "ckn,cqn->ckq", grad_part, right_root, preferred_element_type=jnp.float32
    ).astype(jnp.bfloat16)
    product = jnp.einsum(
        "cpn,cpq->cnq",
        lax.all_gather(left_root, "dp", axis=1, tiled=True),
        half_done,
        preferred_element_type=jnp.float32,
    )
    grad_sq = jnp.sum(jnp.square(grad_part.astype(jnp.float32)), axis=(1, 2))
    prod_sq = lax.psum(jnp.sum(product * product, axis=(1, 2)), "dp")
    cell_count = float(block_width * block_width)
    graft_ratio = jnp.sqrt(grad_sq / cell_count) / jnp.sqrt(prod_sq / cell_count + epsilon)
    scaled = (product * graft_ratio[:, None, None]).astype(jnp.bfloat16)
    returned = lax.all_to_all(
        scaled.reshape(capacity, owners, block_width // owners, quarter),
        "own",
        split_axis=1,
        concat_axis=1,
        tiled=True,
    )
    gathered_back = returned.reshape(capacity * owners, block_width // owners, quarter)
    update = jnp.take(gathered_back, slot_index * owners + owner_list, axis=0)
    return (new_left, new_right, update)


def solution(mesh):
    in_specs = (
        P("dp", None, "own", None),
        P(),
        P("own", "dp", None),
        P("own", "dp", None),
        P("own", "dp", None),
        P("own", "dp", None),
    )
    out_specs = (P("own", "dp", None), P("own", "dp", None), P(None, "own", "dp"))
    return jax.shard_map(body, mesh=mesh, in_specs=in_specs, out_specs=out_specs, check_vma=False)
```

profile of v0, /device:TPU:0, one launch (start us, length us, event | category | flops | bytes accessed | tf_op | source)
XLA Modules:
  0.0 131.5 jit_solution(12707040947900723706)
XLA Ops:
  7.2 0.0 copy-start
  7.2 0.0 all-reduce.2.cloned.1.call-start
  7.2 0.7 all-reduce.2.cloned.1.call-update
  7.9 0.7 fusion.9
  8.7 0.8 select_reduce_fusion
  9.5 0.1 multiply_reduce_fusion.2
  9.6 0.1 reshape.90
  9.7 49.4 %all-reduce.2.cloned.1.call-done = bf16[8,64,512]{2,1,0:T(8,128)(2,1)} async-done(((bf16[8,64,512]{2,1,0:T(8,128)(2,1)}), bf16[8,64,512]{2,1,0:T(8,128)(2,1)}) %all-reduce.2.cloned.1.call-update) | async-done | bytes 524304 | tf_op jit(solution)/shard_map/psum | solution.py:28
  59.1 1.7 %gather_fusion = bf16[16,64,512]{2,1,0:T(8,128)(2,1)S(1)} fusion(bf16[8,64,512]{2,1,0:T(8,128)(2,1)} %all-reduce.2.cloned.1.call-done, s32[1024]{0:T(1024)S(1)} %pad_clamp_fusion.1), kind=kCustom, calls=%fused_computation | custom fusion | bytes 2097216 | tf_op jit(solution)/shard_map/jit(_take)/gather | solution.py:29
  60.7 0.2 select_multiply_fusion
  60.9 1.1 copy.26
  62.0 4.7 %all-to-all-start = ((bf16[2,8,64,512]{3,2,0,1:T(8,128)(2,1)}), bf16[2,8,64,512]{3,2,0,1:T(8,128)(2,1)S(1)}, u32[]{:S(2)}, u32[]{:S(2)}) async-start(bf16[2,8,64,512]{3,2,0,1:T(8,128)(2,1)} %copy.26), calls=%async_computation | async-start | bytes 2097152 | tf_op jit(solution)/shard_map/all_to_all | solution.py:30
  66.8 0.0 all-gather.2.cloned.1.call-start
  66.8 0.7 all-gather.2.cloned.1.call-update
  67.5 0.6 fusion.10
  68.2 0.6 iota_compare_fusion.1
  68.9 24.5 %all-to-all-done = bf16[2,8,64,512]{3,2,0,1:T(8,128)(2,1)S(1)} async-done(((bf16[2,8,64,512]{3,2,0,1:T(8,128)(2,1)}), bf16[2,8,64,512]{3,2,0,1:T(8,128)(2,1)S(1)}, u32[]{:S(2)}, u32[]{:S(2)}) %all-to-all-start) | async-done | bytes 1048608 | tf_op jit(solution)/shard_map/all_to_all | solution.py:30
  93.4 0.1 copy.27
  93.5 3.1 %all-gather.2.cloned.1.call-done = bf16[2,512,512]{2,1,0:T(8,128)(2,1)} async-done(((bf16[2,128,512]{2,1,0:T(8,128)(2,1)}), bf16[2,512,512]{2,1,0:T(8,128)(2,1)}) %all-gather.2.cloned.1.call-update) | async-done | bytes 1048592 | tf_op jit(solution)/shard_map/all_gather | solution.py:50
  96.6 2.1 %multiply_reduce_fusion.1 = (f32[2]{0:T(128)S(1)}, f32[2,128,512]{2,1,0:T(8,128)S(1)}) fusion(bf16[2,512,512]{2,1,0:T(8,128)(2,1)} %all-gather.2.cloned.1.call-done, bf16[2,512,512]{2,1,0:T(8,128)(2,1)S(1)} %bitcast.16, bf16[2,128,512]{2,1,0:T(8,128)(2,1)S(1)} %copy-done), kind=kOutput, calls=%fused_computation.13 | convolution fusion | flops 268828672 | bytes 2883592 | tf_op jit(solution)/shard_map/cpn,cpq->cnq/dot_general | solution.py:48
  98.7 8.9 %psum.15 = f32[2]{0:T(128)S(1)} all-reduce(f32[2]{0:T(128)S(1)} %get-tuple-element.7), channel_id=1, replica_groups=mesh['dp'=4,'own'=8] {'dp'}, use_global_device_ids=true, to_apply=%region_8.9 | all-reduce | flops 2 | bytes 16 | tf_op jit(solution)/shard_map/psum | solution.py:55
  107.6 0.4 multiply_reduce_fusion
  108.0 0.1 fusion.5
  108.1 0.2 copy.30
  108.3 0.7 copy.31
  109.0 4.6 %all-to-all-start.1 = ((bf16[2,8,64,128]{3,2,0,1:T(8,128)(2,1)}), bf16[2,8,64,128]{3,2,0,1:T(8,128)(2,1)S(1)}, u32[]{:S(2)}, u32[]{:S(2)}) async-start(bf16[2,8,64,128]{3,2,0,1:T(8,128)(2,1)} %copy.31), calls=%async_computation.1 | async-start | bytes 524288 | tf_op jit(solution)/shard_map/all_to_all | solution.py:59
  113.6 0.0 copy-start.2
  113.6 1.3 fusion.1
  114.9 1.1 fusion.3
  116.0 7.3 %all-to-all-done.1 = bf16[2,8,64,128]{3,2,0,1:T(8,128)(2,1)S(1)} async-done(((bf16[2,8,64,128]{3,2,0,1:T(8,128)(2,1)}), bf16[2,8,64,128]{3,2,0,1:T(8,128)(2,1)S(1)}, u32[]{:S(2)}, u32[]{:S(2)}) %all-to-all-start.1) | async-done | bytes 262176 | tf_op jit(solution)/shard_map/all_to_all | solution.py:59
  123.4 0.6 gather_fusion.1
  123.9 0.7 broadcast_select_fusion
  (16 shorter events, 0.1 us)
Async XLA Ops:
  7.2 89.4 %copy-start = (bf16[2,128,512]{2,1,0:T(8,128)(2,1)S(1)}, bf16[2,128,512]{2,1,0:T(8,128)(2,1)}, u32[]{:S(2)}) copy-start(bf16[2,128,512]{2,1,0:T(8,128)(2,1)} %param.11) | copy-start | bytes 786436
  7.2 51.9 %all-reduce.2.cloned.1.call-start = ((), (), s32[]{:S(2)}) async-start(), calls=%async_computation.2 | async-start | bytes 1048576 | tf_op jit(solution)/shard_map/psum | solution.py:28
  62.0 5.5 %copy-start.3 = (s32[8]{0:T(128)S(1)}, s32[8]{0:T(128)}, u32[]{:S(2)}) copy-start(s32[8]{0:T(128)} %param.7) | copy-start | bytes 100
  62.0 31.3 %all-to-all-start = ((bf16[2,8,64,512]{3,2,0,1:T(8,128)(2,1)}), bf16[2,8,64,512]{3,2,0,1:T(8,128)(2,1)S(1)}, u32[]{:S(2)}, u32[]{:S(2)}) async-start(bf16[2,8,64,512]{3,2,0,1:T(8,128)(2,1)} %copy.26), calls=%async_computation | async-start | bytes 2097152 | tf_op jit(solution)/shard_map/all_to_all | solution.py:30
  66.8 29.8 %all-gather.2.cloned.1.call-start = ((), (), s32[]{:S(2)}) async-start(), calls=%async_computation.3 | async-start | bytes 1310720 | tf_op jit(solution)/shard_map/all_gather | solution.py:50
  108.0 5.6 %copy-start.1 = (f32[2,128,512]{2,1,0:T(8,128)S(1)}, f32[2,128,512]{2,1,0:T(8,128)}, u32[]{:S(2)}) copy-start(f32[2,128,512]{2,1,0:T(8,128)} %param.8) | copy-start | bytes 1572868
  109.0 14.4 %all-to-all-start.1 = ((bf16[2,8,64,128]{3,2,0,1:T(8,128)(2,1)}), bf16[2,8,64,128]{3,2,0,1:T(8,128)(2,1)S(1)}, u32[]{:S(2)}, u32[]{:S(2)}) async-start(bf16[2,8,64,128]{3,2,0,1:T(8,128)(2,1)} %copy.31), calls=%async_computation.1 | async-start | bytes 524288 | tf_op jit(solution)/shard_map/all_to_all | solution.py:59
  113.6 1.3 copy-start.2
Sparse Core Ops, SparseCore 0:
  11.0 48.0 all-reduce.1
  69.5 27.0 all-gather.1
where the time goes:
time: 132 us
  waiting for transfers between devices  85.7 us (65%)
  between operations  14.2 us (11%)
  starting transfers between devices  9.42 us (7%)
  blocking collectives  8.89 us (7%)
  matrix products  4.5 us (3%)
  other arithmetic  4.44 us (3%)
  local copies, waits for them, and re-layouts  4.42 us (3%)
    psum x1, waiting for transfers between devices, body(): shared = lax.psum(local_terms.astype(jnp.bfloat16), 'dp')  49.4 us
    all_to_all x1, waiting for transfers between devices, body(): lax.all_to_all(outgoing, 'own', split_axis=1, concat_axis=1, tiled=True)  24.5 us
    psum x1, blocking collectives, body(): prod_sq = lax.psum(jnp.sum(product * product, axis=(1, 2)), 'dp')  8.89 us
    all_to_all x1, waiting for transfers between devices, body(): lax.all_to_all(scaled.reshape(capacity, owners, block_width // owners, qu...  7.3 us
    all_to_all x1, starting transfers between devices, body(): lax.all_to_all(outgoing, 'own', split_axis=1, concat_axis=1, tiled=True)  4.74 us
    all_to_all x1, starting transfers between devices, body(): lax.all_to_all(scaled.reshape(capacity, owners, block_width // owners, qu...  4.61 us
    all_gather x1, waiting for transfers between devices, body(): lax.all_gather(left_root, 'dp', axis=1, tiled=True)  3.13 us
  transfers between devices with their start and end apart: 4, of which 4 were waited for; matrix products, arithmetic and copies ran while one was open for 4% of the time, Pallas kernels for 0%

commit v1 on v0

--- a/solution.py
+++ b/solution.py
@@ -1,10 +1,17 @@
+import functools
+
 import jax
 import jax.numpy as jnp
 from jax import lax
+from jax.experimental import pallas as pl
+from jax.experimental.pallas import tpu as pltpu
 from jax.sharding import PartitionSpec as P
 
 decay_rate = 0.95
 epsilon = 1e-06
+
+MESH = pl.DeviceIdType.MESH
+LANES = 128
 
 
 def body(partial_grads, owner_list, left_stat, right_stat, left_root, right_root):
@@ -68,7 +75,352 @@
     return (new_left, new_right, update)
 
 
+def kernel(
+    n_dp,
+    n_own,
+    owner_ref,
+    grads_ref,
+    left_stat_ref,
+    right_stat_ref,
+    left_root_ref,
+    right_root_ref,
+    new_left_ref,
+    new_right_ref,
+    update_ref,
+    parts,
+    summed,
+    routed,
+    grad,
+    left_full,
+    right_quarter,
+    left_old,
+    right_old,
+    sent_back,
+    came_back,
+    norm_sent,
+    norm_came,
+    ratio_all,
+    local_sem,
+    sum_send,
+    sum_recv,
+    root_send,
+    root_recv,
+    route_send,
+    route_recv,
+    spread_send,
+    spread_recv,
+    norm_send,
+    norm_recv,
+    back_send,
+    back_recv,
+    ratio_send,
+    ratio_recv,
+):
+    me = lax.axis_index("dp")
+    own = lax.axis_index("own")
+    blocks, _, rows, width = grads_ref.shape
+    capacity, quarter, _ = left_stat_ref.shape
+    per_quarter = n_own // n_dp
+    dp_of = [lax.rem(me + k, n_dp) for k in range(n_dp)]
+    own_of = [lax.rem(own + k, n_own) for k in range(n_own)]
+
+    def to_dp(k, src, dst, send_sem, recv_sem):
+        return pltpu.make_async_remote_copy(
+            src_ref=src,
+            dst_ref=dst,
+            send_sem=send_sem,
+            recv_sem=recv_sem,
+            device_id=(dp_of[k], own),
+            device_id_type=MESH,
+        )
+
+    def to_own(k, src, dst, send_sem, recv_sem):
+        return pltpu.make_async_remote_copy(
+            src_ref=src,
+            dst_ref=dst,
+            send_sem=send_sem,
+            recv_sem=recv_sem,
+            device_id=(me, own_of[k]),
+            device_id_type=MESH,
+        )
+
+    local = [
+        pltpu.make_async_copy(grads_ref.at[:, me], parts.at[0], local_sem.at[0]),
+        pltpu.make_async_copy(right_root_ref, right_quarter, local_sem.at[1]),
+        pltpu.make_async_copy(left_stat_ref, left_old, local_sem.at[2]),
+        pltpu.make_async_copy(right_stat_ref, right_old, local_sem.at[3]),
+    ]
+    for k in range(n_dp):
+        columns = pl.ds(pl.multiple_of(dp_of[k] * quarter, LANES), quarter)
+        local.append(
+            pltpu.make_async_copy(
+                left_root_ref.at[:, :, columns],
+                left_full.at[:, 0, :, pl.ds(k * quarter, quarter)],
+                local_sem.at[4 + k],
+            )
+        )
+    for copy in local:
+        copy.start()
+
+    barrier = pltpu.get_barrier_semaphore()
+    for k in range(1, n_dp):
+        pl.semaphore_signal(barrier, inc=1, device_id=(dp_of[k], own), device_id_type=MESH)
+    for k in range(1, n_own):
+        pl.semaphore_signal(barrier, inc=1, device_id=(me, own_of[k]), device_id_type=MESH)
+    pl.semaphore_wait(barrier, n_dp - 1 + n_own - 1)
+
+    sums = [
+        to_dp(k, grads_ref.at[:, dp_of[k]], parts.at[k], sum_send.at[k], sum_recv.at[k])
+        for k in range(1, n_dp)
+    ]
+    for copy in sums:
+        copy.start()
+
+    named = [owner_ref[b] for b in range(blocks)]
+    slot_of = []
+    for b in range(blocks):
+        before = jnp.int32(0)
+        for a in range(b):
+            before += (named[a] == named[b]).astype(jnp.int32)
+        slot_of.append(jnp.minimum(before, capacity - 1))
+    source = {}
+    filled = {}
+    for k in range(n_own):
+        for c in range(capacity):
+            source[k, c] = jnp.int32(0)
+            filled[k, c] = jnp.int32(0)
+            for b in range(blocks):
+                hit = jnp.logical_and(named[b] == own_of[k], slot_of[b] == c)
+                source[k, c] = jnp.where(hit, jnp.int32(b), source[k, c])
+                filled[k, c] = jnp.where(hit, jnp.int32(1), filled[k, c])
+
+    local[0].wait()
+    for copy in sums:
+        copy.wait_recv()
+    total = parts[0].astype(jnp.float32)
+    for k in range(1, n_dp):
+        total += parts[k].astype(jnp.float32)
+    summed[...] = total.astype(jnp.bfloat16)
+
+    def pick(k, c):
+        flag = filled[k, c].astype(jnp.float32)
+        return (summed[source[k, c]].astype(jnp.float32) * flag).astype(jnp.bfloat16)
+
+    routes = {}
+    for k in range(1, n_own):
+        for c in range(capacity):
+            routed[k, c] = pick(k, c)
+        routes[k] = to_own(
+            k, routed.at[k], grad.at[:, own, me], route_send.at[k], route_recv.at[k]
+        )
+        routes[k].start()
+    for c in range(capacity):
+        grad[c, own, me] = pick(0, c)
+
+    roots = []
+    for k in range(1, n_dp):
+        at = n_dp - k
+        nxt = at % (n_dp - 1) + 1
+        for j, column in enumerate((at, nxt)):
+            whole = lax.rem(dp_of[k] + column, n_dp)
+            columns = pl.ds(pl.multiple_of(whole * quarter, LANES), quarter)
+            roots.append(
+                to_dp(
+                    k,
+                    left_root_ref.at[:, :, columns],
+                    left_full.at[:, at, :, pl.ds(column * quarter, quarter)],
+                    root_send.at[k, j],
+                    root_recv.at[k, j],
+                )
+            )
+    for copy in roots:
+        copy.start()
+
+    spreads = []
+    for k in range(n_own):
+        if k:
+            routes[k].wait_recv()
+        piece = lax.rem(own + n_own - k, n_own)
+        for j in range(1, n_dp):
+            copy = to_dp(
+                j,
+                grad.at[:, piece, me],
+                grad.at[:, piece, me],
+                spread_send.at[k, j],
+                spread_recv.at[k, j],
+            )
+            copy.start()
+            spreads.append(copy)
+
+    for copy in local[1:]:
+        copy.wait()
+    for copy in roots:
+        copy.wait_recv()
+    for c in range(capacity):
+        for k in range(1, n_dp):
+            nxt = k % (n_dp - 1) + 1
+            left_full[c, k, :, pl.ds(0, quarter)] = left_full[
+                c, 0, :, pl.ds(k * quarter, quarter)
+            ].T
+            left_full[c, nxt, :, pl.ds(k * quarter, quarter)] = left_full[
+                c, k, :, pl.ds(nxt * quarter, quarter)
+            ].T
+
+    for copy in spreads:
+        copy.wait_recv()
+
+    cells = float(width * width)
+    nt = (((1,), (1,)), ((), ()))
+    tn = (((0,), (0,)), ((), ()))
+
+    def grad_rows(c, k):
+        return grad[c, pl.ds(dp_of[k] * per_quarter, per_quarter)].reshape(quarter, width)
+
+    for c in range(capacity):
+        half = jnp.concatenate(
+            [
+                lax.dot_general(
+                    grad_rows(c, k), right_quarter[c], nt, preferred_element_type=jnp.float32
+                ).astype(jnp.bfloat16)
+                for k in range(n_dp)
+            ],
+            axis=0,
+        )
+        product = jnp.dot(
+            left_full[c].reshape(width, width), half, preferred_element_type=jnp.float32
+        )
+        for k in range(n_dp):
+            piece = product[k * quarter : (k + 1) * quarter].astype(jnp.bfloat16)
+            for j in range(per_quarter):
+                step = quarter // per_quarter
+                sent_back[dp_of[k] * per_quarter + j, c] = piece[j * step : (j + 1) * step]
+        norm_sent[c] = jnp.sum(jnp.square(product).reshape(width // 8, 8, quarter), axis=0)
+    norms = [
+        to_dp(k, norm_sent, norm_came.at[k], norm_send.at[k], norm_recv.at[k])
+        for k in range(1, n_dp)
+    ]
+    for copy in norms:
+        copy.start()
+    backs = [
+        to_own(
+            k, sent_back.at[own_of[k]], came_back.at[own], back_send.at[k], back_recv.at[k]
+        )
+        for k in range(1, n_own)
+    ]
+    for copy in backs:
+        copy.start()
+    came_back[own] = sent_back[own]
+
+    grad_sq = []
+    for c in range(capacity):
+        squares = jnp.square(grad[c].reshape(width, width).astype(jnp.float32))
+        grad_sq.append(jnp.sum(squares.reshape(width // 8, 8, width), axis=0))
+    for copy in norms:
+        copy.wait_recv()
+    for c in range(capacity):
+        prod_sq = norm_sent[c]
+        for k in range(1, n_dp):
+            prod_sq += norm_came[k, c]
+        prod_all = jnp.sum(prod_sq, keepdims=True).reshape(1, 1)
+        grad_all = jnp.sum(grad_sq[c], keepdims=True).reshape(1, 1)
+        ratio = jnp.sqrt(grad_all / cells) / jnp.sqrt(prod_all / cells + epsilon)
+        ratio_all[own, c] = jnp.broadcast_to(ratio, (8, LANES))
+    ratios = [
+        to_own(k, ratio_all.at[own], ratio_all.at[own], ratio_send.at[k], ratio_recv.at[k])
+        for k in range(1, n_own)
+    ]
+    for copy in ratios:
+        copy.start()
+
+    for c in range(capacity):
+        used = filled[0, c].astype(jnp.float32)
+        decay = 1.0 - used * (1.0 - decay_rate)
+        whole = grad[c].reshape(width, width)
+        left_gram = lax.dot_general(
+            grad_rows(c, 0), whole, nt, preferred_element_type=jnp.float32
+        )
+        new_left_ref[c] = decay * left_old[c] + left_gram * (1.0 / width)
+        columns = pl.ds(pl.multiple_of(me * quarter, LANES), quarter)
+        mine = grad[c, :, :, :, columns].reshape(width, quarter)
+        right_gram = lax.dot_general(mine, whole, tn, preferred_element_type=jnp.float32)
+        new_right_ref[c] = decay * right_old[c] + right_gram * (1.0 / width)
+
+    for copy in backs:
+        copy.wait_recv()
+    for copy in ratios:
+        copy.wait_recv()
+    for b in range(blocks):
+        ratio = ratio_all[named[b], slot_of[b]][0:1, :]
+        terms = came_back[named[b], slot_of[b]].astype(jnp.float32)
+        update_ref[b] = (terms * ratio).astype(jnp.bfloat16)
+
+    for copy in sums + roots + spreads + norms + backs + ratios:
+        copy.wait_send()
+    for k in routes:
+        routes[k].wait_send()
+
+
+def fused(n_dp, n_own, partial_grads, owner_list, left_stat, right_stat, left_root, right_root):
+    capacity, quarter, width = left_stat.shape
+    blocks, strip = partial_grads.shape[1:3]
+    rows = strip // n_dp
+    bf16, f32 = jnp.bfloat16, jnp.float32
+    dma = pltpu.SemaphoreType.DMA
+    anywhere = pl.BlockSpec(memory_space=pl.ANY)
+    return pl.pallas_call(
+        functools.partial(kernel, n_dp, n_own),
+        out_shape=(
+            jax.ShapeDtypeStruct(left_stat.shape, f32),
+            jax.ShapeDtypeStruct(right_stat.shape, f32),
+            jax.ShapeDtypeStruct((blocks, strip, quarter), bf16),
+        ),
+        in_specs=[pl.BlockSpec(memory_space=pltpu.SMEM)] + [anywhere] * 5,
+        out_specs=tuple([pl.BlockSpec(memory_space=pltpu.VMEM)] * 3),
+        scratch_shapes=[
+            pltpu.VMEM((n_dp, blocks, rows, width), bf16),
+            pltpu.VMEM((blocks, rows, width), bf16),
+            pltpu.VMEM((n_own, capacity, rows, width), bf16),
+            pltpu.VMEM((capacity, n_own, n_dp, rows, width), bf16),
+            pltpu.VMEM((capacity, n_dp, quarter, width), bf16),
+            pltpu.VMEM((capacity, quarter, width), bf16),
+            pltpu.VMEM((capacity, quarter, width), f32),
+            pltpu.VMEM((capacity, quarter, width), f32),
+            pltpu.VMEM((n_own, capacity, strip, quarter), bf16),
+            pltpu.VMEM((n_own, capacity, strip, quarter), bf16),
+            pltpu.VMEM((capacity, 8, LANES), f32),
+            pltpu.VMEM((n_dp, capacity, 8, LANES), f32),
+            pltpu.VMEM((n_own, capacity, 8, LANES), f32),
+            dma((4 + n_dp,)),
+            dma((n_dp,)),
+            dma((n_dp,)),
+            dma((n_dp, 2)),
+            dma((n_dp, 2)),
+            dma((n_own,)),
+            dma((n_own,)),
+            dma((n_own, n_dp)),
+            dma((n_own, n_dp)),
+            dma((n_dp,)),
+            dma((n_dp,)),
+            dma((n_own,)),
+            dma((n_own,)),
+            dma((n_own,)),
+            dma((n_own,)),
+        ],
+        compiler_params=pltpu.CompilerParams(
+            collective_id=0, has_side_effects=True, vmem_limit_bytes=40 * 1024 * 1024
+        ),
+    )(
+        owner_list,
+        partial_grads[0].reshape(blocks, n_dp, rows, width),
+        left_stat,
+        right_stat,
+        left_root,
+        right_root,
+    )
+
+
 def solution(mesh):
+    n_dp, n_own = mesh.shape["dp"], mesh.shape["own"]
     in_specs = (
         P("dp", None, "own", None),
         P(),
@@ -78,4 +430,19 @@
         P("own", "dp", None),
     )
     out_specs = (P("own", "dp", None), P("own", "dp", None), P(None, "own", "dp"))
-    return jax.shard_map(body, mesh=mesh, in_specs=in_specs, out_specs=out_specs, check_vma=False)
+
+    def step(*operands):
+        strip = operands[0].shape[2]
+        quarter = operands[2].shape[1]
+        fits = (
+            n_dp == 4
+            and n_own % n_dp == 0
+            and strip % (16 * n_dp) == 0
+            and quarter == LANES
+            and strip * n_own == quarter * n_dp
+        )
+        if fits:
+            return fused(n_dp, n_own, *operands)
+        return body(*operands)
+
+    return jax.shard_map(step, mesh=mesh, in_specs=in_specs, out_specs=out_specs, check_vma=False)

time: 132 us -> 51.8 us (0.39)
  waiting for transfers between devices: 85.7 us -> 0 us
  Pallas kernels: 0 us -> 42.9 us
  between operations: 14.2 us -> 0.65 us
  starting transfers between devices: 9.42 us -> 0 us
  blocking collectives: 8.89 us -> 0 us
  matrix products: 4.5 us -> 0 us
  other arithmetic: 4.44 us -> 0 us
  local copies, waits for them, and re-layouts: 4.42 us -> 7.91 us
    psum x1 -> x0, waiting for transfers between devices: 49.4 us -> none  [body(): shared = lax.psum(local_terms.astype(jnp.bfloat16), 'dp')]
    pallas_call x0 -> x1, Pallas kernels: none -> 42.9 us  [fused(): pl.pallas_call(functools.partial(kernel, n_dp, n_own), out_shape=(jax.Sha...]
    all_to_all x2 -> x0, waiting for transfers between devices: 31.8 us -> none  [the longest x1 24.5 us: body(): lax.all_to_all(outgoing, 'own', split_axis=1, concat_axis=1, tiled=True)]
    all_to_all x2 -> x0, starting transfers between devices: 9.34 us -> none  [the longest x1 4.74 us: body(): lax.all_to_all(outgoing, 'own', split_axis=1, concat_axis=1, tiled=True)]
    psum x1 -> x0, blocking collectives: 8.89 us -> none  [body(): prod_sq = lax.psum(jnp.sum(product * product, axis=(1, 2)), 'dp')]
    unnamed x8 -> x15, local copies, waits for them, and re-layouts: 0.02 us -> 7.91 us
    dot_general x3 -> x0, matrix products: 4.5 us -> none  [the longest x1 2.08 us: body(): jnp.einsum('cpn,cpq->cnq', lax.all_gather(left_root, 'dp', axis=1, tiled=...]
    all_gather x1 -> x0, waiting for transfers between devices: 3.13 us -> none  [body(): lax.all_gather(left_root, 'dp', axis=1, tiled=True)]
  transfers between devices with their start and end apart: 4 -> 0, of which waited for: 4 -> 0; matrix products, arithmetic and copies ran while one was open for 4% -> 0% of each run, Pallas kernels for 0% -> 0%
where the time goes in v1:
time: 51.8 us; the launch traced here: 51.5 us
  Pallas kernels  42.9 us (83%)
  local copies, waits for them, and re-layouts  7.91 us (15%)
  between operations  0.65 us (1%)
    pallas_call x1, Pallas kernels, fused(): pl.pallas_call(functools.partial(kernel, n_dp, n_own), out_shape=(jax.Sha...  42.9 us
    unnamed x15, local copies, waits for them, and re-layouts  7.91 us

profile of v1, /device:TPU:0, one launch (start us, length us, event | category | flops | bytes accessed | tf_op | source)
XLA Modules:
  0.0 51.5 jit_solution(15266485745174391576)
XLA Ops:
  0.6 0.0 copy-start.5
  0.6 0.6 %copy-done.5 = s32[8]{0:T(128)S(1)} copy-done((s32[8]{0:T(128)S(1)}, s32[8]{0:T(128)}, u32[]{:S(2)}) %copy-start.5) | copy-done | bytes 56
  1.3 0.0 copy-start
  1.3 1.0 %copy-done = bf16[1,8,64,512]{3,2,1,0:T(8,128)(2,1)S(1)} copy-done((bf16[1,8,64,512]{3,2,1,0:T(8,128)(2,1)S(1)}, bf16[1,8,64,512]{3,2,1,0:T(8,128)(2,1)}, u32[]{:S(2)}) %copy-start) | copy-done | bytes 524312
  2.3 0.0 copy-start.1
  2.3 1.0 %copy-done.1 = f32[2,128,512]{2,1,0:T(8,128)S(1)} copy-done((f32[2,128,512]{2,1,0:T(8,128)S(1)}, f32[2,128,512]{2,1,0:T(8,128)}, u32[]{:S(2)}) %copy-start.1) | copy-done | bytes 524312
  3.4 0.0 copy-start.2
  3.4 1.0 %copy-done.2 = f32[2,128,512]{2,1,0:T(8,128)S(1)} copy-done((f32[2,128,512]{2,1,0:T(8,128)S(1)}, f32[2,128,512]{2,1,0:T(8,128)}, u32[]{:S(2)}) %copy-start.2) | copy-done | bytes 524312
  4.4 0.0 copy-start.3
  4.4 0.9 %copy-done.3 = bf16[2,128,512]{2,1,0:T(8,128)(2,1)S(1)} copy-done((bf16[2,128,512]{2,1,0:T(8,128)(2,1)S(1)}, bf16[2,128,512]{2,1,0:T(8,128)(2,1)}, u32[]{:S(2)}) %copy-start.3) | copy-done | bytes 262168
  5.4 0.0 copy-start.4
  5.4 0.9 %copy-done.4 = bf16[2,128,512]{2,1,0:T(8,128)(2,1)S(1)} copy-done((bf16[2,128,512]{2,1,0:T(8,128)(2,1)S(1)}, bf16[2,128,512]{2,1,0:T(8,128)(2,1)}, u32[]{:S(2)}) %copy-start.4) | copy-done | bytes 262168
  6.3 42.9 %shard_map.85 = (f32[2,128,512]{2,1,0:T(8,128)S(1)}, f32[2,128,512]{2,1,0:T(8,128)S(1)}, bf16[8,64,128]{2,1,0:T(8,128)(2,1)S(1)}) custom-call(s32[8]{0:T(128)S(1)} %copy-done.5, bf16[8,4,16,512]{3,2,1,0:T(8,128)(2,1)S(1)} %bitcast.1, f32[2,128,512]{2,1,0:T(8,128)S(1)} %copy-done.1, f32[2,128,512]{2,1,0:T(8,128)S(1)} %copy-done.2, ...), custom_call_target="tpu_custom_call" | custom-call | tf_op jit(solution)/shard_map/pallas_call | solution.py:370
  49.2 0.8 %copy.12 = f32[2,128,512]{2,1,0:T(8,128)} copy(f32[2,128,512]{2,1,0:T(8,128)S(1)} %get-tuple-element.6) | data formatting | bytes 1048576
  50.0 0.8 %copy.13 = f32[2,128,512]{2,1,0:T(8,128)} copy(f32[2,128,512]{2,1,0:T(8,128)S(1)} %get-tuple-element.7) | data formatting | bytes 1048576
  50.8 0.7 %copy.14 = bf16[8,64,128]{2,1,0:T(8,128)(2,1)} copy(bf16[8,64,128]{2,1,0:T(8,128)(2,1)S(1)} %get-tuple-element.8) | data formatting | bytes 262144
Async XLA Ops:
  0.6 0.7 %copy-start.5 = (s32[8]{0:T(128)S(1)}, s32[8]{0:T(128)}, u32[]{:S(2)}) copy-start(s32[8]{0:T(128)} %owner_ref.1) | copy-start | bytes 100
  1.3 1.0 %copy-start = (bf16[1,8,64,512]{3,2,1,0:T(8,128)(2,1)S(1)}, bf16[1,8,64,512]{3,2,1,0:T(8,128)(2,1)}, u32[]{:S(2)}) copy-start(bf16[1,8,64,512]{3,2,1,0:T(8,128)(2,1)} %param.6) | copy-start | bytes 1572868
  2.3 1.0 %copy-start.1 = (f32[2,128,512]{2,1,0:T(8,128)S(1)}, f32[2,128,512]{2,1,0:T(8,128)}, u32[]{:S(2)}) copy-start(f32[2,128,512]{2,1,0:T(8,128)} %left_stat_ref.1) | copy-start | bytes 1572868
  3.4 1.0 %copy-start.2 = (f32[2,128,512]{2,1,0:T(8,128)S(1)}, f32[2,128,512]{2,1,0:T(8,128)}, u32[]{:S(2)}) copy-start(f32[2,128,512]{2,1,0:T(8,128)} %right_stat_ref.1) | copy-start | bytes 1572868
  4.4 0.9 %copy-start.3 = (bf16[2,128,512]{2,1,0:T(8,128)(2,1)S(1)}, bf16[2,128,512]{2,1,0:T(8,128)(2,1)}, u32[]{:S(2)}) copy-start(bf16[2,128,512]{2,1,0:T(8,128)(2,1)} %left_root_ref.1) | copy-start | bytes 786436
  5.4 0.9 %copy-start.4 = (bf16[2,128,512]{2,1,0:T(8,128)(2,1)S(1)}, bf16[2,128,512]{2,1,0:T(8,128)(2,1)}, u32[]{:S(2)}) copy-start(bf16[2,128,512]{2,1,0:T(8,128)(2,1)} %right_root_ref.1) | copy-start | bytes 786436

commit v2 on v1

--- a/solution.py
+++ b/solution.py
@@ -176,6 +176,25 @@
     for copy in sums:
         copy.start()
 
+    roots = []
+    for j in range(2):
+        for k in range(1, n_dp):
+            at = n_dp - k
+            column = (at, at % (n_dp - 1) + 1)[j]
+            whole = lax.rem(dp_of[k] + column, n_dp)
+            columns = pl.ds(pl.multiple_of(whole * quarter, LANES), quarter)
+            roots.append(
+                to_dp(
+                    k,
+                    left_root_ref.at[:, :, columns],
+                    left_full.at[:, at, :, pl.ds(column * quarter, quarter)],
+                    root_send.at[k, j],
+                    root_recv.at[k, j],
+                )
+            )
+    for copy in roots[: n_dp - 1]:
+        copy.start()
+
     named = [owner_ref[b] for b in range(blocks)]
     slot_of = []
     for b in range(blocks):
@@ -207,50 +226,37 @@
         return (summed[source[k, c]].astype(jnp.float32) * flag).astype(jnp.bfloat16)
 
     routes = {}
-    for k in range(1, n_own):
-        for c in range(capacity):
+    for c in range(capacity):
+        for k in range(1, n_own):
             routed[k, c] = pick(k, c)
-        routes[k] = to_own(
-            k, routed.at[k], grad.at[:, own, me], route_send.at[k], route_recv.at[k]
-        )
-        routes[k].start()
-    for c in range(capacity):
+            routes[c, k] = to_own(
+                k,
+                routed.at[k, c],
+                grad.at[c, own, me],
+                route_send.at[c, k],
+                route_recv.at[c, k],
+            )
+            routes[c, k].start()
         grad[c, own, me] = pick(0, c)
-
-    roots = []
-    for k in range(1, n_dp):
-        at = n_dp - k
-        nxt = at % (n_dp - 1) + 1
-        for j, column in enumerate((at, nxt)):
-            whole = lax.rem(dp_of[k] + column, n_dp)
-            columns = pl.ds(pl.multiple_of(whole * quarter, LANES), quarter)
-            roots.append(
-                to_dp(
-                    k,
-                    left_root_ref.at[:, :, columns],
-                    left_full.at[:, at, :, pl.ds(column * quarter, quarter)],
-                    root_send.at[k, j],
-                    root_recv.at[k, j],
+    for copy in roots[n_dp - 1 :]:
+        copy.start()
+
+    spreads = {}
+    for c in range(capacity):
+        for k in range(n_own):
+            if k:
+                routes[c, k].wait_recv()
+            piece = lax.rem(own + n_own - k, n_own)
+            for j in range(1, n_dp):
+                copy = to_dp(
+                    j,
+                    grad.at[c, piece, me],
+                    grad.at[c, piece, me],
+                    spread_send.at[c, k, j],
+                    spread_recv.at[c, k, j],
                 )
-            )
-    for copy in roots:
-        copy.start()
-
-    spreads = []
-    for k in range(n_own):
-        if k:
-            routes[k].wait_recv()
-        piece = lax.rem(own + n_own - k, n_own)
-        for j in range(1, n_dp):
-            copy = to_dp(
-                j,
-                grad.at[:, piece, me],
-                grad.at[:, piece, me],
-                spread_send.at[k, j],
-                spread_recv.at[k, j],
-            )
-            copy.start()
-            spreads.append(copy)
+                copy.start()
+                spreads[c, k, j] = copy
 
     for copy in local[1:]:
         copy.wait()
@@ -266,9 +272,6 @@
                 c, k, :, pl.ds(nxt * quarter, quarter)
             ].T
 
-    for copy in spreads:
-        copy.wait_recv()
-
     cells = float(width * width)
     nt = (((1,), (1,)), ((), ()))
     tn = (((0,), (0,)), ((), ()))
@@ -276,7 +279,13 @@
     def grad_rows(c, k):
         return grad[c, pl.ds(dp_of[k] * per_quarter, per_quarter)].reshape(quarter, width)
 
-    for c in range(capacity):
+    norms = {}
+    backs = {}
+    ratios = {}
+    for c in range(capacity):
+        for k in range(n_own):
+            for j in range(1, n_dp):
+                spreads[c, k, j].wait_recv()
         half = jnp.concatenate(
             [
                 lax.dot_general(
@@ -293,44 +302,40 @@
             piece = product[k * quarter : (k + 1) * quarter].astype(jnp.bfloat16)
             for j in range(per_quarter):
                 step = quarter // per_quarter
-                sent_back[dp_of[k] * per_quarter + j, c] = piece[j * step : (j + 1) * step]
+                sent_back[c, dp_of[k] * per_quarter + j] = piece[j * step : (j + 1) * step]
         norm_sent[c] = jnp.sum(jnp.square(product).reshape(width // 8, 8, quarter), axis=0)
-    norms = [
-        to_dp(k, norm_sent, norm_came.at[k], norm_send.at[k], norm_recv.at[k])
-        for k in range(1, n_dp)
-    ]
-    for copy in norms:
-        copy.start()
-    backs = [
-        to_own(
-            k, sent_back.at[own_of[k]], came_back.at[own], back_send.at[k], back_recv.at[k]
-        )
-        for k in range(1, n_own)
-    ]
-    for copy in backs:
-        copy.start()
-    came_back[own] = sent_back[own]
-
-    grad_sq = []
+        for k in range(1, n_dp):
+            norms[c, k] = to_dp(
+                k, norm_sent.at[c], norm_came.at[c, k], norm_send.at[c, k], norm_recv.at[c, k]
+            )
+            norms[c, k].start()
+        for k in range(1, n_own):
+            backs[c, k] = to_own(
+                k,
+                sent_back.at[c, own_of[k]],
+                came_back.at[c, own],
+                back_send.at[c, k],
+                back_recv.at[c, k],
+            )
+            backs[c, k].start()
+        came_back[c, own] = sent_back[c, own]
+
     for c in range(capacity):
         squares = jnp.square(grad[c].reshape(width, width).astype(jnp.float32))
-        grad_sq.append(jnp.sum(squares.reshape(width // 8, 8, width), axis=0))
-    for copy in norms:
-        copy.wait_recv()
-    for c in range(capacity):
+        grad_sq = jnp.sum(squares.reshape(width // 8, 8, width), axis=0)
         prod_sq = norm_sent[c]
         for k in range(1, n_dp):
-            prod_sq += norm_came[k, c]
+            norms[c, k].wait_recv()
+            prod_sq += norm_came[c, k]
         prod_all = jnp.sum(prod_sq, keepdims=True).reshape(1, 1)
-        grad_all = jnp.sum(grad_sq[c], keepdims=True).reshape(1, 1)
+        grad_all = jnp.sum(grad_sq, keepdims=True).reshape(1, 1)
         ratio = jnp.sqrt(grad_all / cells) / jnp.sqrt(prod_all / cells + epsilon)
         ratio_all[own, c] = jnp.broadcast_to(ratio, (8, LANES))
-    ratios = [
-        to_own(k, ratio_all.at[own], ratio_all.at[own], ratio_send.at[k], ratio_recv.at[k])
-        for k in range(1, n_own)
-    ]
-    for copy in ratios:
-        copy.start()
+    for k in range(1, n_own):
+        ratios[k] = to_own(
+            k, ratio_all.at[own], ratio_all.at[own], ratio_send.at[k], ratio_recv.at[k]
+        )
+        ratios[k].start()
 
     for c in range(capacity):
         used = filled[0, c].astype(jnp.float32)
@@ -345,19 +350,18 @@
         right_gram = lax.dot_general(mine, whole, tn, preferred_element_type=jnp.float32)
         new_right_ref[c] = decay * right_old[c] + right_gram * (1.0 / width)
 
-    for copy in backs:
-        copy.wait_recv()
-    for copy in ratios:
+    for copy in [*backs.values(), *ratios.values()]:
         copy.wait_recv()
     for b in range(blocks):
         ratio = ratio_all[named[b], slot_of[b]][0:1, :]
-        terms = came_back[named[b], slot_of[b]].astype(jnp.float32)
+        terms = came_back[slot_of[b], named[b]].astype(jnp.float32)
         update_ref[b] = (terms * ratio).astype(jnp.bfloat16)
 
-    for copy in sums + roots + spreads + norms + backs + ratios:
+    for copy in sums + roots:
         copy.wait_send()
-    for k in routes:
-        routes[k].wait_send()
+    for group in (routes, spreads, norms, backs, ratios):
+        for copy in group.values():
+            copy.wait_send()
 
 
 def fused(n_dp, n_own, partial_grads, owner_list, left_stat, right_stat, left_root, right_root):
@@ -366,7 +370,7 @@
     rows = strip // n_dp
     bf16, f32 = jnp.bfloat16, jnp.float32
     dma = pltpu.SemaphoreType.DMA
-    anywhere = pl.BlockSpec(memory_space=pl.ANY)
+    anywhere = pl.BlockSpec(memory_space=pltpu.HBM)
     return pl.pallas_call(
         functools.partial(kernel, n_dp, n_own),
         out_shape=(
@@ -385,29 +389,29 @@
             pltpu.VMEM((capacity, quarter, width), bf16),
             pltpu.VMEM((capacity, quarter, width), f32),
             pltpu.VMEM((capacity, quarter, width), f32),
-            pltpu.VMEM((n_own, capacity, strip, quarter), bf16),
-            pltpu.VMEM((n_own, capacity, strip, quarter), bf16),
+            pltpu.VMEM((capacity, n_own, strip, quarter), bf16),
+            pltpu.VMEM((capacity, n_own, strip, quarter), bf16),
             pltpu.VMEM((capacity, 8, LANES), f32),
-            pltpu.VMEM((n_dp, capacity, 8, LANES), f32),
+            pltpu.VMEM((capacity, n_dp, 8, LANES), f32),
             pltpu.VMEM((n_own, capacity, 8, LANES), f32),
             dma((4 + n_dp,)),
             dma((n_dp,)),
             dma((n_dp,)),
             dma((n_dp, 2)),
             dma((n_dp, 2)),
-            dma((n_own,)),
-            dma((n_own,)),
-            dma((n_own, n_dp)),
-            dma((n_own, n_dp)),
-            dma((n_dp,)),
-            dma((n_dp,)),
-            dma((n_own,)),
-            dma((n_own,)),
+            dma((capacity, n_own)),
+            dma((capacity, n_own)),
+            dma((capacity, n_own, n_dp)),
+            dma((capacity, n_own, n_dp)),
+            dma((capacity, n_dp)),
+            dma((capacity, n_dp)),
+            dma((capacity, n_own)),
+            dma((capacity, n_own)),
             dma((n_own,)),
             dma((n_own,)),
         ],
         compiler_params=pltpu.CompilerParams(
-            collective_id=0, has_side_effects=True, vmem_limit_bytes=40 * 1024 * 1024
+            collective_id=0, has_side_effects=True, vmem_limit_bytes=62 * 1024 * 1024
         ),
     )(
         owner_list,

time: 51.8 us -> 46.3 us (0.89)
  local copies, waits for them, and re-layouts: 7.91 us -> 3.61 us
  Pallas kernels: 42.9 us -> 41.8 us
    unnamed x15 -> x7, local copies, waits for them, and re-layouts: 7.91 us -> 3.61 us
    pallas_call x1, Pallas kernels: 42.9 us -> 41.8 us  [fused(): pl.pallas_call(functools.partial(kernel, n_dp, n_own), out_shape=(jax.Sha...]
where the time goes in v2:
time: 46.3 us; the launch traced here: 46.1 us
  Pallas kernels  41.8 us (90%)
  local copies, waits for them, and re-layouts  3.61 us (8%)
  between operations  0.65 us (1%)
    pallas_call x1, Pallas kernels, fused(): pl.pallas_call(functools.partial(kernel, n_dp, n_own), out_shape=(jax.Sha...  41.8 us
    unnamed x7, local copies, waits for them, and re-layouts  3.61 us

profile of v2, /device:TPU:0, one launch (start us, length us, event | category | flops | bytes accessed | tf_op | source)
XLA Modules:
  0.0 46.1 jit_solution(17873611969717671904)
XLA Ops:
  0.6 41.8 %shard_map.85 = (f32[2,128,512]{2,1,0:T(8,128)}, f32[2,128,512]{2,1,0:T(8,128)}, bf16[8,64,128]{2,1,0:T(8,128)(2,1)}) custom-call(s32[8]{0:T(128)} %owner_ref.1, bf16[8,4,16,512]{3,2,1,0:T(8,128)(2,1)} %bitcast.1, f32[2,128,512]{2,1,0:T(8,128)} %left_stat_ref.1, f32[2,128,512]{2,1,0:T(8,128)} %right_stat_ref.1, bf16[2,128,512]{2,1,0:T(8,128)(2,1)} %left_root_ref.1, ...), custom_call_target="tpu_custom_call" | custom-call | tf_op jit(solution)/shard_map/pallas_call | solution.py:374
  42.5 0.0 copy-start
  42.5 1.9 %copy.12 = f32[2,128,512]{2,1,0:T(8,128)} copy(f32[2,128,512]{2,1,0:T(8,128)} %get-tuple-element.6) | data formatting | bytes 1048576
  44.4 0.0 copy-done
  44.4 0.0 copy-start.1
  44.4 0.8 %copy.13 = f32[2,128,512]{2,1,0:T(8,128)} copy(f32[2,128,512]{2,1,0:T(8,128)S(1)} %copy-done) | data formatting | bytes 1048576
  45.2 0.2 copy-done.1
  45.4 0.7 %copy.14 = bf16[8,64,128]{2,1,0:T(8,128)(2,1)} copy(bf16[8,64,128]{2,1,0:T(8,128)(2,1)S(1)} %copy-done.1) | data formatting | bytes 262144
Async XLA Ops:
  42.5 1.9 %copy-start = (f32[2,128,512]{2,1,0:T(8,128)S(1)}, f32[2,128,512]{2,1,0:T(8,128)}, u32[]{:S(2)}) copy-start(f32[2,128,512]{2,1,0:T(8,128)} %get-tuple-element.7) | copy-start | bytes 1572868
  44.4 1.0 %copy-start.1 = (bf16[8,64,128]{2,1,0:T(8,128)(2,1)S(1)}, bf16[8,64,128]{2,1,0:T(8,128)(2,1)}, u32[]{:S(2)}) copy-start(bf16[8,64,128]{2,1,0:T(8,128)(2,1)} %get-tuple-element.8) | copy-start | bytes 393220

commit v3 on v2

--- a/solution.py
+++ b/solution.py
@@ -121,7 +121,7 @@
     blocks, _, rows, width = grads_ref.shape
     capacity, quarter, _ = left_stat_ref.shape
     per_quarter = n_own // n_dp
-    dp_of = [lax.rem(me + k, n_dp) for k in range(n_dp)]
+    dp_of = [me, me + 1 - 2 * (me % 2), me + 2 - 4 * (me // 2), 3 - me]
     own_of = [lax.rem(own + k, n_own) for k in range(n_own)]
 
     def to_dp(k, src, dst, send_sem, recv_sem):
@@ -179,15 +179,13 @@
     roots = []
     for j in range(2):
         for k in range(1, n_dp):
-            at = n_dp - k
-            column = (at, at % (n_dp - 1) + 1)[j]
-            whole = lax.rem(dp_of[k] + column, n_dp)
-            columns = pl.ds(pl.multiple_of(whole * quarter, LANES), quarter)
+            column = (k, k % (n_dp - 1) + 1)[j]
+            columns = pl.ds(pl.multiple_of(dp_of[k ^ column] * quarter, LANES), quarter)
             roots.append(
                 to_dp(
                     k,
                     left_root_ref.at[:, :, columns],
-                    left_full.at[:, at, :, pl.ds(column * quarter, quarter)],
+                    left_full.at[:, k, :, pl.ds(column * quarter, quarter)],
                     root_send.at[k, j],
                     root_recv.at[k, j],
                 )
@@ -242,21 +240,37 @@
         copy.start()
 
     spreads = {}
-    for c in range(capacity):
-        for k in range(n_own):
-            if k:
-                routes[c, k].wait_recv()
-            piece = lax.rem(own + n_own - k, n_own)
-            for j in range(1, n_dp):
-                copy = to_dp(
-                    j,
-                    grad.at[c, piece, me],
-                    grad.at[c, piece, me],
-                    spread_send.at[c, k, j],
-                    spread_recv.at[c, k, j],
-                )
-                copy.start()
-                spreads[c, k, j] = copy
+    arrived = set()
+
+    def spread(c, k, j, source_at):
+        piece = lax.rem(own + n_own - k, n_own)
+        across = 3 if source_at else j
+        spreads[c, k, across] = to_dp(
+            j,
+            grad.at[c, piece, dp_of[source_at]],
+            grad.at[c, piece, dp_of[source_at]],
+            spread_send.at[c, k, across],
+            spread_recv.at[c, k, across],
+        )
+        spreads[c, k, across].start()
+
+    def relay(c, k):
+        came = 1 + (c + k) % 2
+        spreads[c, k, came].wait_recv()
+        arrived.add((c, k, came))
+        spread(c, k, 3 - came, came)
+
+    lag = 3
+    order = [(c, k) for c in range(capacity) for k in range(n_own)]
+    for at, (c, k) in enumerate(order):
+        if k:
+            routes[c, k].wait_recv()
+        spread(c, k, 1, 0)
+        spread(c, k, 2, 0)
+        if at >= lag:
+            relay(*order[at - lag])
+    for c, k in order[-lag:]:
+        relay(c, k)
 
     for copy in local[1:]:
         copy.wait()
@@ -285,7 +299,8 @@
     for c in range(capacity):
         for k in range(n_own):
             for j in range(1, n_dp):
-                spreads[c, k, j].wait_recv()
+                if (c, k, j) not in arrived:
+                    spreads[c, k, j].wait_recv()
         half = jnp.concatenate(
             [
                 lax.dot_general(
@@ -364,6 +379,17 @@
             copy.wait_send()
 
 
+def write_out(*refs):
+    inputs, outputs, sems = refs[:3], refs[3:6], refs[6]
+    copies = [
+        pltpu.make_async_copy(inputs[i], outputs[i], sems.at[i]) for i in range(len(inputs))
+    ]
+    for copy in copies:
+        copy.start()
+    for copy in copies:
+        copy.wait()
+
+
 def fused(n_dp, n_own, partial_grads, owner_list, left_stat, right_stat, left_root, right_root):
     capacity, quarter, width = left_stat.shape
     blocks, strip = partial_grads.shape[1:3]
@@ -371,13 +397,12 @@
     bf16, f32 = jnp.bfloat16, jnp.float32
     dma = pltpu.SemaphoreType.DMA
     anywhere = pl.BlockSpec(memory_space=pltpu.HBM)
-    return pl.pallas_call(
+    hbm = functools.partial(pltpu.with_memory_space_constraint, memory_space=pltpu.HBM)
+    shapes = (left_stat.shape, right_stat.shape, (blocks, strip, quarter))
+    types = (f32, f32, bf16)
+    results = pl.pallas_call(
         functools.partial(kernel, n_dp, n_own),
-        out_shape=(
-            jax.ShapeDtypeStruct(left_stat.shape, f32),
-            jax.ShapeDtypeStruct(right_stat.shape, f32),
-            jax.ShapeDtypeStruct((blocks, strip, quarter), bf16),
-        ),
+        out_shape=tuple(pltpu.VMEM(shape, kind) for shape, kind in zip(shapes, types)),
         in_specs=[pl.BlockSpec(memory_space=pltpu.SMEM)] + [anywhere] * 5,
         out_specs=tuple([pl.BlockSpec(memory_space=pltpu.VMEM)] * 3),
         scratch_shapes=[
@@ -411,16 +436,23 @@
             dma((n_own,)),
         ],
         compiler_params=pltpu.CompilerParams(
-            collective_id=0, has_side_effects=True, vmem_limit_bytes=62 * 1024 * 1024
+            collective_id=0, has_side_effects=True, vmem_limit_bytes=40 * 1024 * 1024
         ),
     )(
-        owner_list,
-        partial_grads[0].reshape(blocks, n_dp, rows, width),
-        left_stat,
-        right_stat,
-        left_root,
-        right_root,
-    )
+        hbm(owner_list),
+        hbm(partial_grads[0].reshape(blocks, n_dp, rows, width)),
+        hbm(left_stat),
+        hbm(right_stat),
+        hbm(left_root),
+        hbm(right_root),
+    )
+    return pl.pallas_call(
+        write_out,
+        out_shape=tuple(jax.ShapeDtypeStruct(shape, kind) for shape, kind in zip(shapes, types)),
+        in_specs=[pl.BlockSpec(memory_space=pltpu.VMEM)] * 3,
+        out_specs=tuple([pl.BlockSpec(memory_space=pltpu.HBM)] * 3),
+        scratch_shapes=[dma((3,))],
+    )(*results)
 
 
 def solution(mesh):

time: 46.3 us -> 48.4 us (1.045)
  Pallas kernels: 41.8 us -> 45.4 us
  local copies, waits for them, and re-layouts: 3.61 us -> 2.21 us
    pallas_call x1 -> x2, Pallas kernels: 41.8 us -> 45.4 us  [the longest x1 43.2 us: fused(): pl.pallas_call(functools.partial(kernel, n_dp, n_own), out_shape=tuple((p...]
    unnamed x7 -> x6, local copies, waits for them, and re-layouts: 3.61 us -> 2.21 us
where the time goes in v3:
time: 48.4 us; the launch traced here: 48.3 us
  Pallas kernels  45.4 us (94%)
  local copies, waits for them, and re-layouts  2.21 us (5%)
  between operations  0.65 us (1%)
    pallas_call x1, Pallas kernels, fused(): pl.pallas_call(functools.partial(kernel, n_dp, n_own), out_shape=tuple((p...  43.2 us
    pallas_call x1, Pallas kernels, fused(): pl.pallas_call(write_out, out_shape=tuple((jax.ShapeDtypeStruct(shape, ki...  2.24 us
    unnamed x6, local copies, waits for them, and re-layouts  2.21 us

profile of v3, /device:TPU:0, one launch (start us, length us, event | category | flops | bytes accessed | tf_op | source)
XLA Modules:
  0.0 48.3 jit_solution(5670429501013230633)
XLA Ops:
  0.6 43.2 %shard_map.85 = (f32[2,128,512]{2,1,0:T(8,128)S(1)}, f32[2,128,512]{2,1,0:T(8,128)S(1)}, bf16[8,64,128]{2,1,0:T(8,128)(2,1)S(1)}) custom-call(s32[8]{0:T(128)} %owner_ref.1, bf16[8,4,16,512]{3,2,1,0:T(8,128)(2,1)} %bitcast.1, f32[2,128,512]{2,1,0:T(8,128)} %left_stat_ref.1, f32[2,128,512]{2,1,0:T(8,128)} %right_stat_ref.1, ...), custom_call_target="tpu_custom_call" | custom-call | tf_op jit(solution)/shard_map/pallas_call | solution.py:403
  43.8 0.0 copy-start
  43.8 0.8 %copy-done = f32[2,128,512]{2,1,0:T(8,128)} copy-done((f32[2,128,512]{2,1,0:T(8,128)}, f32[2,128,512]{2,1,0:T(8,128)S(1)}, u32[]{:S(2)}) %copy-start) | copy-done | bytes 524312
  44.6 0.0 copy-start.1
  44.6 0.8 %copy-done.1 = f32[2,128,512]{2,1,0:T(8,128)} copy-done((f32[2,128,512]{2,1,0:T(8,128)}, f32[2,128,512]{2,1,0:T(8,128)S(1)}, u32[]{:S(2)}) %copy-start.1) | copy-done | bytes 524312
  45.4 0.0 copy-start.2
  45.4 0.6 %copy-done.2 = bf16[8,64,128]{2,1,0:T(8,128)(2,1)} copy-done((bf16[8,64,128]{2,1,0:T(8,128)(2,1)}, bf16[8,64,128]{2,1,0:T(8,128)(2,1)S(1)}, u32[]{:S(2)}) %copy-start.2) | copy-done | bytes 131096
  46.0 2.2 %shard_map.86 = (f32[2,128,512]{2,1,0:T(8,128)}, f32[2,128,512]{2,1,0:T(8,128)}, bf16[8,64,128]{2,1,0:T(8,128)(2,1)}) custom-call(f32[2,128,512]{2,1,0:T(8,128)} %copy-done, f32[2,128,512]{2,1,0:T(8,128)} %copy-done.1, bf16[8,64,128]{2,1,0:T(8,128)(2,1)} %copy-done.2), custom_call_target="tpu_custom_call" | custom-call | tf_op jit(solution)/shard_map/pallas_call | solution.py:449
Async XLA Ops:
  43.8 0.8 %copy-start = (f32[2,128,512]{2,1,0:T(8,128)}, f32[2,128,512]{2,1,0:T(8,128)S(1)}, u32[]{:S(2)}) copy-start(f32[2,128,512]{2,1,0:T(8,128)S(1)} %get-tuple-element.6.refs_0_) | copy-start | bytes 1572868
  44.6 0.8 %copy-start.1 = (f32[2,128,512]{2,1,0:T(8,128)}, f32[2,128,512]{2,1,0:T(8,128)S(1)}, u32[]{:S(2)}) copy-start(f32[2,128,512]{2,1,0:T(8,128)S(1)} %get-tuple-element.7.refs_1_) | copy-start | bytes 1572868
  45.4 0.6 %copy-start.2 = (bf16[8,64,128]{2,1,0:T(8,128)(2,1)}, bf16[8,64,128]{2,1,0:T(8,128)(2,1)S(1)}, u32[]{:S(2)}) copy-start(bf16[8,64,128]{2,1,0:T(8,128)(2,1)S(1)} %get-tuple-element.8.refs_2_) | copy-start | bytes 393220

commit v4 on v3

--- a/solution.py
+++ b/solution.py
@@ -101,20 +101,8 @@
     norm_came,
     ratio_all,
     local_sem,
-    sum_send,
-    sum_recv,
-    root_send,
-    root_recv,
-    route_send,
-    route_recv,
-    spread_send,
-    spread_recv,
-    norm_send,
-    norm_recv,
-    back_send,
-    back_recv,
-    ratio_send,
-    ratio_recv,
+    send_sem,
+    recv_sem,
 ):
     me = lax.axis_index("dp")
     own = lax.axis_index("own")
@@ -124,25 +112,38 @@
     dp_of = [me, me + 1 - 2 * (me % 2), me + 2 - 4 * (me // 2), 3 - me]
     own_of = [lax.rem(own + k, n_own) for k in range(n_own)]
 
-    def to_dp(k, src, dst, send_sem, recv_sem):
-        return pltpu.make_async_remote_copy(
+    def send(src, dst, group, c, device):
+        pltpu.make_async_remote_copy(
             src_ref=src,
             dst_ref=dst,
-            send_sem=send_sem,
-            recv_sem=recv_sem,
-            device_id=(dp_of[k], own),
+            send_sem=send_sem.at[group, c],
+            recv_sem=recv_sem.at[group, c],
+            device_id=device,
             device_id_type=MESH,
-        )
-
-    def to_own(k, src, dst, send_sem, recv_sem):
-        return pltpu.make_async_remote_copy(
-            src_ref=src,
-            dst_ref=dst,
-            send_sem=send_sem,
-            recv_sem=recv_sem,
-            device_id=(me, own_of[k]),
-            device_id_type=MESH,
-        )
+        ).start()
+
+    def to_dp(k, src, dst, group, c):
+        send(src, dst, group, c, (dp_of[k], own))
+
+    def to_own(k, src, dst, group, c):
+        send(src, dst, group, c, (me, own_of[k]))
+
+    def wait_for(sem, like):
+        pltpu.make_async_copy(like, like, sem).wait()
+
+    sums, roots, routes, spreads, norms, backs, ratios = range(7)
+    sizes = {
+        sums: parts.at[pl.ds(1, n_dp - 1)],
+        roots: left_full.at[:, pl.ds(1, n_dp - 1), :, pl.ds(0, 2 * quarter)],
+        routes: grad.at[0, pl.ds(1, n_own - 1), 0],
+        spreads: grad.at[0, :, pl.ds(1, n_dp - 1)],
+        norms: norm_came.at[0, pl.ds(1, n_dp - 1)],
+        backs: came_back.at[0, pl.ds(1, n_own - 1)],
+        ratios: ratio_all.at[pl.ds(1, n_own - 1)],
+    }
+
+    def arrived(group, c=0):
+        wait_for(recv_sem.at[group, c], sizes[group])
 
     local = [
         pltpu.make_async_copy(grads_ref.at[:, me], parts.at[0], local_sem.at[0]),
@@ -169,29 +170,8 @@
         pl.semaphore_signal(barrier, inc=1, device_id=(me, own_of[k]), device_id_type=MESH)
     pl.semaphore_wait(barrier, n_dp - 1 + n_own - 1)
 
-    sums = [
-        to_dp(k, grads_ref.at[:, dp_of[k]], parts.at[k], sum_send.at[k], sum_recv.at[k])
-        for k in range(1, n_dp)
-    ]
-    for copy in sums:
-        copy.start()
-
-    roots = []
-    for j in range(2):
-        for k in range(1, n_dp):
-            column = (k, k % (n_dp - 1) + 1)[j]
-            columns = pl.ds(pl.multiple_of(dp_of[k ^ column] * quarter, LANES), quarter)
-            roots.append(
-                to_dp(
-                    k,
-                    left_root_ref.at[:, :, columns],
-                    left_full.at[:, k, :, pl.ds(column * quarter, quarter)],
-                    root_send.at[k, j],
-                    root_recv.at[k, j],
-                )
-            )
-    for copy in roots[: n_dp - 1]:
-        copy.start()
+    for k in range(1, n_dp):
+        to_dp(k, grads_ref.at[:, dp_of[k]], parts.at[k], sums, 0)
 
     named = [owner_ref[b] for b in range(blocks)]
     slot_of = []
@@ -212,8 +192,7 @@
                 filled[k, c] = jnp.where(hit, jnp.int32(1), filled[k, c])
 
     local[0].wait()
-    for copy in sums:
-        copy.wait_recv()
+    arrived(sums)
     total = parts[0].astype(jnp.float32)
     for k in range(1, n_dp):
         total += parts[k].astype(jnp.float32)
@@ -223,59 +202,31 @@
         flag = filled[k, c].astype(jnp.float32)
         return (summed[source[k, c]].astype(jnp.float32) * flag).astype(jnp.bfloat16)
 
-    routes = {}
     for c in range(capacity):
         for k in range(1, n_own):
             routed[k, c] = pick(k, c)
-            routes[c, k] = to_own(
+            to_own(k, routed.at[k, c], grad.at[c, own, me], routes, c)
+        grad[c, own, me] = pick(0, c)
+
+    for k in range(1, n_dp):
+        for column in (k, k % (n_dp - 1) + 1):
+            columns = pl.ds(pl.multiple_of(dp_of[k ^ column] * quarter, LANES), quarter)
+            to_dp(
                 k,
-                routed.at[k, c],
-                grad.at[c, own, me],
-                route_send.at[c, k],
-                route_recv.at[c, k],
+                left_root_ref.at[:, :, columns],
+                left_full.at[:, k, :, pl.ds(column * quarter, quarter)],
+                roots,
+                0,
             )
-            routes[c, k].start()
-        grad[c, own, me] = pick(0, c)
-    for copy in roots[n_dp - 1 :]:
-        copy.start()
-
-    spreads = {}
-    arrived = set()
-
-    def spread(c, k, j, source_at):
-        piece = lax.rem(own + n_own - k, n_own)
-        across = 3 if source_at else j
-        spreads[c, k, across] = to_dp(
-            j,
-            grad.at[c, piece, dp_of[source_at]],
-            grad.at[c, piece, dp_of[source_at]],
-            spread_send.at[c, k, across],
-            spread_recv.at[c, k, across],
-        )
-        spreads[c, k, across].start()
-
-    def relay(c, k):
-        came = 1 + (c + k) % 2
-        spreads[c, k, came].wait_recv()
-        arrived.add((c, k, came))
-        spread(c, k, 3 - came, came)
-
-    lag = 3
-    order = [(c, k) for c in range(capacity) for k in range(n_own)]
-    for at, (c, k) in enumerate(order):
-        if k:
-            routes[c, k].wait_recv()
-        spread(c, k, 1, 0)
-        spread(c, k, 2, 0)
-        if at >= lag:
-            relay(*order[at - lag])
-    for c, k in order[-lag:]:
-        relay(c, k)
+
+    for c in range(capacity):
+        arrived(routes, c)
+        for k in range(1, n_dp):
+            to_dp(k, grad.at[c, :, me], grad.at[c, :, me], spreads, c)
 
     for copy in local[1:]:
         copy.wait()
-    for copy in roots:
-        copy.wait_recv()
+    arrived(roots)
     for c in range(capacity):
         for k in range(1, n_dp):
             nxt = k % (n_dp - 1) + 1
@@ -293,14 +244,21 @@
     def grad_rows(c, k):
         return grad[c, pl.ds(dp_of[k] * per_quarter, per_quarter)].reshape(quarter, width)
 
-    norms = {}
-    backs = {}
-    ratios = {}
-    for c in range(capacity):
-        for k in range(n_own):
-            for j in range(1, n_dp):
-                if (c, k, j) not in arrived:
-                    spreads[c, k, j].wait_recv()
+    def statistics(c):
+        used = filled[0, c].astype(jnp.float32)
+        decay = 1.0 - used * (1.0 - decay_rate)
+        whole = grad[c].reshape(width, width)
+        left_gram = lax.dot_general(
+            grad_rows(c, 0), whole, nt, preferred_element_type=jnp.float32
+        )
+        new_left_ref[c] = decay * left_old[c] + left_gram * (1.0 / width)
+        columns = pl.ds(pl.multiple_of(me * quarter, LANES), quarter)
+        mine = grad[c, :, :, :, columns].reshape(width, quarter)
+        right_gram = lax.dot_general(mine, whole, tn, preferred_element_type=jnp.float32)
+        new_right_ref[c] = decay * right_old[c] + right_gram * (1.0 / width)
+
+    for c in range(capacity):
+        arrived(spreads, c)
         half = jnp.concatenate(
             [
                 lax.dot_general(
@@ -320,63 +278,39 @@
                 sent_back[c, dp_of[k] * per_quarter + j] = piece[j * step : (j + 1) * step]
         norm_sent[c] = jnp.sum(jnp.square(product).reshape(width // 8, 8, quarter), axis=0)
         for k in range(1, n_dp):
-            norms[c, k] = to_dp(
-                k, norm_sent.at[c], norm_came.at[c, k], norm_send.at[c, k], norm_recv.at[c, k]
-            )
-            norms[c, k].start()
+            to_dp(k, norm_sent.at[c], norm_came.at[c, k], norms, c)
         for k in range(1, n_own):
-            backs[c, k] = to_own(
-                k,
-                sent_back.at[c, own_of[k]],
-                came_back.at[c, own],
-                back_send.at[c, k],
-                back_recv.at[c, k],
-            )
-            backs[c, k].start()
+            to_own(k, sent_back.at[c, own_of[k]], came_back.at[c, own], backs, c)
         came_back[c, own] = sent_back[c, own]
+        if c < capacity - 1:
+            statistics(c)
 
     for c in range(capacity):
         squares = jnp.square(grad[c].reshape(width, width).astype(jnp.float32))
         grad_sq = jnp.sum(squares.reshape(width // 8, 8, width), axis=0)
+        arrived(norms, c)
         prod_sq = norm_sent[c]
         for k in range(1, n_dp):
-            norms[c, k].wait_recv()
             prod_sq += norm_came[c, k]
         prod_all = jnp.sum(prod_sq, keepdims=True).reshape(1, 1)
         grad_all = jnp.sum(grad_sq, keepdims=True).reshape(1, 1)
         ratio = jnp.sqrt(grad_all / cells) / jnp.sqrt(prod_all / cells + epsilon)
         ratio_all[own, c] = jnp.broadcast_to(ratio, (8, LANES))
     for k in range(1, n_own):
-        ratios[k] = to_own(
-            k, ratio_all.at[own], ratio_all.at[own], ratio_send.at[k], ratio_recv.at[k]
-        )
-        ratios[k].start()
-
-    for c in range(capacity):
-        used = filled[0, c].astype(jnp.float32)
-        decay = 1.0 - used * (1.0 - decay_rate)
-        whole = grad[c].reshape(width, width)
-        left_gram = lax.dot_general(
-            grad_rows(c, 0), whole, nt, preferred_element_type=jnp.float32
-        )
-        new_left_ref[c] = decay * left_old[c] + left_gram * (1.0 / width)
-        columns = pl.ds(pl.multiple_of(me * quarter, LANES), quarter)
-        mine = grad[c, :, :, :, columns].reshape(width, quarter)
-        right_gram = lax.dot_general(mine, whole, tn, preferred_element_type=jnp.float32)
-        new_right_ref[c] = decay * right_old[c] + right_gram * (1.0 / width)
-
-    for copy in [*backs.values(), *ratios.values()]:
-        copy.wait_recv()
+        to_own(k, ratio_all.at[own], ratio_all.at[own], ratios, 0)
+    statistics(capacity - 1)
+
+    for c in range(capacity):
+        arrived(backs, c)
+    arrived(ratios)
     for b in range(blocks):
         ratio = ratio_all[named[b], slot_of[b]][0:1, :]
         terms = came_back[slot_of[b], named[b]].astype(jnp.float32)
         update_ref[b] = (terms * ratio).astype(jnp.bfloat16)
 
-    for copy in sums + roots:
-        copy.wait_send()
-    for group in (routes, spreads, norms, backs, ratios):
-        for copy in group.values():
-            copy.wait_send()
+    for group in sizes:
+        for c in range(1 if group in (sums, roots, ratios) else capacity):
+            wait_for(send_sem.at[group, c], sizes[group])
 
 
 def write_out(*refs):
@@ -396,7 +330,7 @@
     rows = strip // n_dp
     bf16, f32 = jnp.bfloat16, jnp.float32
     dma = pltpu.SemaphoreType.DMA
-    anywhere = pl.BlockSpec(memory_space=pltpu.HBM)
+    anywhere = pl.BlockSpec(memory_space=pl.ANY)
     hbm = functools.partial(pltpu.with_memory_space_constraint, memory_space=pltpu.HBM)
     shapes = (left_stat.shape, right_stat.shape, (blocks, strip, quarter))
     types = (f32, f32, bf16)
@@ -420,20 +354,8 @@
             pltpu.VMEM((capacity, n_dp, 8, LANES), f32),
             pltpu.VMEM((n_own, capacity, 8, LANES), f32),
             dma((4 + n_dp,)),
-            dma((n_dp,)),
-            dma((n_dp,)),
-            dma((n_dp, 2)),
-            dma((n_dp, 2)),
-            dma((capacity, n_own)),
-            dma((capacity, n_own)),
-            dma((capacity, n_own, n_dp)),
-            dma((capacity, n_own, n_dp)),
-            dma((capacity, n_dp)),
-            dma((capacity, n_dp)),
-            dma((capacity, n_own)),
-            dma((capacity, n_own)),
-            dma((n_own,)),
-            dma((n_own,)),
+            dma((7, capacity)),
+            dma((7, capacity)),
         ],
         compiler_params=pltpu.CompilerParams(
             collective_id=0, has_side_effects=True, vmem_limit_bytes=40 * 1024 * 1024
@@ -449,10 +371,11 @@
     return pl.pallas_call(
         write_out,
         out_shape=tuple(jax.ShapeDtypeStruct(shape, kind) for shape, kind in zip(shapes, types)),
-        in_specs=[pl.BlockSpec(memory_space=pltpu.VMEM)] * 3,
+        in_specs=[anywhere] * 3,
         out_specs=tuple([pl.BlockSpec(memory_space=pltpu.HBM)] * 3),
         scratch_shapes=[dma((3,))],
-    )(*results)
+        compiler_params=pltpu.CompilerParams(vmem_limit_bytes=4 * 1024 * 1024),
+    )(*[pltpu.with_memory_space_constraint(x, pltpu.VMEM) for x in results])
 
 
 def solution(mesh):

time: 48.4 us -> 44.3 us (0.915)
  local copies, waits for them, and re-layouts: 2.21 us -> 0 us
  Pallas kernels: 45.4 us -> 43.5 us
    unnamed x6 -> x0, local copies, waits for them, and re-layouts: 2.21 us -> none
    pallas_call x1, Pallas kernels: 2.24 us -> 1.03 us  [fused(): pl.pallas_call(write_out, out_shape=tuple((jax.ShapeDtypeStruct(shape, ki...]
    pallas_call x1, Pallas kernels: 43.2 us -> 42.5 us  [fused(): pl.pallas_call(functools.partial(kernel, n_dp, n_own), out_shape=tuple((p...]
where the time goes in v4:
time: 44.3 us; the launch traced here: 44.1 us
  Pallas kernels  43.5 us (98%)
  between operations  0.64 us (1%)
    pallas_call x1, Pallas kernels, fused(): pl.pallas_call(functools.partial(kernel, n_dp, n_own), out_shape=tuple((p...  42.5 us
    pallas_call x1, Pallas kernels, fused(): pl.pallas_call(write_out, out_shape=tuple((jax.ShapeDtypeStruct(shape, ki...  1.03 us

profile of v4, /device:TPU:0, one launch (start us, length us, event | category | flops | bytes accessed | tf_op | source)
XLA Modules:
  0.0 44.1 jit_solution(17452498891352834768)
XLA Ops:
  0.6 42.5 %shard_map.85 = (f32[2,128,512]{2,1,0:T(8,128)S(1)}, f32[2,128,512]{2,1,0:T(8,128)S(1)}, bf16[8,64,128]{2,1,0:T(8,128)(2,1)S(1)}) custom-call(s32[8]{0:T(128)} %owner_ref.1, bf16[8,4,16,512]{3,2,1,0:T(8,128)(2,1)} %bitcast.1, f32[2,128,512]{2,1,0:T(8,128)} %left_stat_ref.1, f32[2,128,512]{2,1,0:T(8,128)} %right_stat_ref.1, ...), custom_call_target="tpu_custom_call" | custom-call | tf_op jit(solution)/shard_map/pallas_call | solution.py:337
  43.1 1.0 %shard_map.86 = (f32[2,128,512]{2,1,0:T(8,128)}, f32[2,128,512]{2,1,0:T(8,128)}, bf16[8,64,128]{2,1,0:T(8,128)(2,1)}) custom-call(f32[2,128,512]{2,1,0:T(8,128)S(1)} %get-tuple-element.6.refs_0_, f32[2,128,512]{2,1,0:T(8,128)S(1)} %get-tuple-element.7.refs_1_, bf16[8,64,128]{2,1,0:T(8,128)(2,1)S(1)} %get-tuple-element.8.refs_2_), custom_call_target="tpu_custom_call" | custom-call | tf_op jit(solution)/shard_map/pallas_call | solution.py:371

commit v5 on v4

--- a/solution.py
+++ b/solution.py
@@ -103,6 +103,8 @@
     local_sem,
     send_sem,
     recv_sem,
+    spread_send,
+    spread_recv,
 ):
     me = lax.axis_index("dp")
     own = lax.axis_index("own")
@@ -110,7 +112,11 @@
     capacity, quarter, _ = left_stat_ref.shape
     per_quarter = n_own // n_dp
     dp_of = [me, me + 1 - 2 * (me % 2), me + 2 - 4 * (me // 2), 3 - me]
-    own_of = [lax.rem(own + k, n_own) for k in range(n_own)]
+    near = n_own // 2
+    base = (own // near) * near
+    turn = own - base
+    own_of = [base + lax.rem(turn + k, near) for k in range(near)]
+    own_of += [near - base + lax.rem(turn + k, near) for k in range(near)]
 
     def send(src, dst, group, c, device):
         pltpu.make_async_remote_copy(
@@ -131,12 +137,12 @@
     def wait_for(sem, like):
         pltpu.make_async_copy(like, like, sem).wait()
 
-    sums, roots, routes, spreads, norms, backs, ratios = range(7)
+    sums, roots, routes_near, routes_far, norms, backs, ratios = range(7)
     sizes = {
         sums: parts.at[pl.ds(1, n_dp - 1)],
         roots: left_full.at[:, pl.ds(1, n_dp - 1), :, pl.ds(0, 2 * quarter)],
-        routes: grad.at[0, pl.ds(1, n_own - 1), 0],
-        spreads: grad.at[0, :, pl.ds(1, n_dp - 1)],
+        routes_near: grad.at[0, pl.ds(1, near - 1), 0],
+        routes_far: grad.at[0, pl.ds(0, near), 0],
         norms: norm_came.at[0, pl.ds(1, n_dp - 1)],
         backs: came_back.at[0, pl.ds(1, n_own - 1)],
         ratios: ratio_all.at[pl.ds(1, n_own - 1)],
@@ -172,6 +178,22 @@
 
     for k in range(1, n_dp):
         to_dp(k, grads_ref.at[:, dp_of[k]], parts.at[k], sums, 0)
+
+    def send_root(k, column, slots):
+        columns = pl.ds(pl.multiple_of(dp_of[k ^ column] * quarter, LANES), quarter)
+        to_dp(
+            k,
+            left_root_ref.at[slots, :, columns],
+            left_full.at[slots, k, :, pl.ds(column * quarter, quarter)],
+            roots,
+            0,
+        )
+
+    every = pl.ds(0, capacity)
+    root_pieces = [(1, 1, every), (2, 2, every), (3, 3, every), (1, 3, every), (2, 3, every)]
+    root_pieces += [(1 + c % 2, 2 - c % 2, pl.ds(c, 1)) for c in range(capacity)]
+    for copy in root_pieces[: n_dp - 1]:
+        send_root(*copy)
 
     named = [owner_ref[b] for b in range(blocks)]
     slot_of = []
@@ -205,37 +227,59 @@
     for c in range(capacity):
         for k in range(1, n_own):
             routed[k, c] = pick(k, c)
-            to_own(k, routed.at[k, c], grad.at[c, own, me], routes, c)
+            group = routes_near if k < near else routes_far
+            to_own(k, routed.at[k, c], grad.at[c, own, me], group, c)
         grad[c, own, me] = pick(0, c)
 
-    for k in range(1, n_dp):
-        for column in (k, k % (n_dp - 1) + 1):
-            columns = pl.ds(pl.multiple_of(dp_of[k ^ column] * quarter, LANES), quarter)
-            to_dp(
-                k,
-                left_root_ref.at[:, :, columns],
-                left_full.at[:, k, :, pl.ds(column * quarter, quarter)],
-                roots,
-                0,
-            )
-
-    for c in range(capacity):
-        arrived(routes, c)
-        for k in range(1, n_dp):
-            to_dp(k, grad.at[c, :, me], grad.at[c, :, me], spreads, c)
+    for copy in root_pieces[n_dp - 1 :]:
+        send_root(*copy)
+
+    def half_of(c, far, at):
+        start = near - base if far else base
+        return grad.at[c, pl.ds(start, near), dp_of[at]]
+
+    def spread(c, far, k, at):
+        piece = half_of(c, far, at)
+        across = k ^ at
+        pltpu.make_async_remote_copy(
+            src_ref=piece,
+            dst_ref=piece,
+            send_sem=spread_send.at[c, far, across],
+            recv_sem=spread_recv.at[c, far, across],
+            device_id=(dp_of[k], own),
+            device_id_type=MESH,
+        ).start()
+
+    def spread_arrived(c, far, at):
+        wait_for(spread_recv.at[c, far, at], half_of(c, far, at))
+
+    def start_spread(c, far):
+        arrived(routes_far if far else routes_near, c)
+        for k in (2, 1) if far else (1, 2):
+            spread(c, far, k, 0)
+
+    def relay(c, far):
+        came = 2 if far else 1
+        spread_arrived(c, far, came)
+        spread(c, far, 3 - came, came)
+
+    halves = [(c, far) for c in range(capacity) for far in range(2)]
+    lag = 2
+    for at, half in enumerate(halves):
+        start_spread(*half)
+        if at >= lag:
+            relay(*halves[at - lag])
 
     for copy in local[1:]:
         copy.wait()
     arrived(roots)
     for c in range(capacity):
-        for k in range(1, n_dp):
-            nxt = k % (n_dp - 1) + 1
-            left_full[c, k, :, pl.ds(0, quarter)] = left_full[
-                c, 0, :, pl.ds(k * quarter, quarter)
+        for i, j in ((0, 1), (0, 2), (0, 3), (1, 3), (2, 3), (1 + c % 2, 2 - c % 2)):
+            left_full[c, j, :, pl.ds(i * quarter, quarter)] = left_full[
+                c, i, :, pl.ds(j * quarter, quarter)
             ].T
-            left_full[c, nxt, :, pl.ds(k * quarter, quarter)] = left_full[
-                c, k, :, pl.ds(nxt * quarter, quarter)
-            ].T
+    for half in halves[-lag:]:
+        relay(*half)
 
     cells = float(width * width)
     nt = (((1,), (1,)), ((), ()))
@@ -258,7 +302,9 @@
         new_right_ref[c] = decay * right_old[c] + right_gram * (1.0 / width)
 
     for c in range(capacity):
-        arrived(spreads, c)
+        for far in range(2):
+            spread_arrived(c, far, 1 if far else 2)
+            spread_arrived(c, far, 3)
         half = jnp.concatenate(
             [
                 lax.dot_general(
@@ -279,11 +325,9 @@
         norm_sent[c] = jnp.sum(jnp.square(product).reshape(width // 8, 8, quarter), axis=0)
         for k in range(1, n_dp):
             to_dp(k, norm_sent.at[c], norm_came.at[c, k], norms, c)
-        for k in range(1, n_own):
+        for k in reversed(range(1, n_own)):
             to_own(k, sent_back.at[c, own_of[k]], came_back.at[c, own], backs, c)
         came_back[c, own] = sent_back[c, own]
-        if c < capacity - 1:
-            statistics(c)
 
     for c in range(capacity):
         squares = jnp.square(grad[c].reshape(width, width).astype(jnp.float32))
@@ -298,7 +342,8 @@
         ratio_all[own, c] = jnp.broadcast_to(ratio, (8, LANES))
     for k in range(1, n_own):
         to_own(k, ratio_all.at[own], ratio_all.at[own], ratios, 0)
-    statistics(capacity - 1)
+    for c in range(capacity):
+        statistics(c)
 
     for c in range(capacity):
         arrived(backs, c)
@@ -311,6 +356,9 @@
     for group in sizes:
         for c in range(1 if group in (sums, roots, ratios) else capacity):
             wait_for(send_sem.at[group, c], sizes[group])
+    for c, far in halves:
+        for k in range(1, n_dp):
+            wait_for(spread_send.at[c, far, k], half_of(c, far, 0))
 
 
 def write_out(*refs):
@@ -356,6 +404,8 @@
             dma((4 + n_dp,)),
             dma((7, capacity)),
             dma((7, capacity)),
+            dma((capacity, 2, n_dp)),
+            dma((capacity, 2, n_dp)),
         ],
         compiler_params=pltpu.CompilerParams(
             collective_id=0, has_side_effects=True, vmem_limit_bytes=40 * 1024 * 1024
@@ -396,6 +446,7 @@
         fits = (
             n_dp == 4
             and n_own % n_dp == 0
+            and n_own >= 2 * n_dp
             and strip % (16 * n_dp) == 0
             and quarter == LANES
             and strip * n_own == quarter * n_dp

time: 44.3 us -> 42.3 us (0.955)
  Pallas kernels: 43.5 us -> 41.5 us
    pallas_call x1, Pallas kernels: 42.5 us -> 40.5 us  [fused(): pl.pallas_call(functools.partial(kernel, n_dp, n_own), out_shape=tuple((p...]
where the time goes in v5:
time: 42.3 us; the launch traced here: 42.2 us
  Pallas kernels  41.5 us (98%)
  between operations  0.64 us (2%)
    pallas_call x1, Pallas kernels, fused(): pl.pallas_call(functools.partial(kernel, n_dp, n_own), out_shape=tuple((p...  40.5 us
    pallas_call x1, Pallas kernels, fused(): pl.pallas_call(write_out, out_shape=tuple((jax.ShapeDtypeStruct(shape, ki...  1.03 us

profile of v5, /device:TPU:0, one launch (start us, length us, event | category | flops | bytes accessed | tf_op | source)
XLA Modules:
  0.0 42.2 jit_solution(631529458717804641)
XLA Ops:
  0.6 40.5 %shard_map.85 = (f32[2,128,512]{2,1,0:T(8,128)S(1)}, f32[2,128,512]{2,1,0:T(8,128)S(1)}, bf16[8,64,128]{2,1,0:T(8,128)(2,1)S(1)}) custom-call(s32[8]{0:T(128)} %owner_ref.1, bf16[8,4,16,512]{3,2,1,0:T(8,128)(2,1)} %bitcast.1, f32[2,128,512]{2,1,0:T(8,128)} %left_stat_ref.1, f32[2,128,512]{2,1,0:T(8,128)} %right_stat_ref.1, ...), custom_call_target="tpu_custom_call" | custom-call | tf_op jit(solution)/shard_map/pallas_call | solution.py:385
  41.2 1.0 %shard_map.86 = (f32[2,128,512]{2,1,0:T(8,128)}, f32[2,128,512]{2,1,0:T(8,128)}, bf16[8,64,128]{2,1,0:T(8,128)(2,1)}) custom-call(f32[2,128,512]{2,1,0:T(8,128)S(1)} %get-tuple-element.6.refs_0_, f32[2,128,512]{2,1,0:T(8,128)S(1)} %get-tuple-element.7.refs_1_, bf16[8,64,128]{2,1,0:T(8,128)(2,1)S(1)} %get-tuple-element.8.refs_2_), custom_call_target="tpu_custom_call" | custom-call | tf_op jit(solution)/shard_map/pallas_call | solution.py:421

commit v6 on v5

--- a/solution.py
+++ b/solution.py
@@ -145,7 +145,7 @@
         routes_far: grad.at[0, pl.ds(0, near), 0],
         norms: norm_came.at[0, pl.ds(1, n_dp - 1)],
         backs: came_back.at[0, pl.ds(1, n_own - 1)],
-        ratios: ratio_all.at[pl.ds(1, n_own - 1)],
+        ratios: ratio_all.at[0, pl.ds(1, n_own - 1)],
     }
 
     def arrived(group, c=0):
@@ -166,8 +166,7 @@
                 local_sem.at[4 + k],
             )
         )
-    for copy in local:
-        copy.start()
+    local[0].start()
 
     barrier = pltpu.get_barrier_semaphore()
     for k in range(1, n_dp):
@@ -176,7 +175,7 @@
         pl.semaphore_signal(barrier, inc=1, device_id=(me, own_of[k]), device_id_type=MESH)
     pl.semaphore_wait(barrier, n_dp - 1 + n_own - 1)
 
-    for k in range(1, n_dp):
+    for k in reversed(range(1, n_dp)):
         to_dp(k, grads_ref.at[:, dp_of[k]], parts.at[k], sums, 0)
 
     def send_root(k, column, slots):
@@ -224,15 +223,18 @@
         flag = filled[k, c].astype(jnp.float32)
         return (summed[source[k, c]].astype(jnp.float32) * flag).astype(jnp.bfloat16)
 
+    for group, first, last in ((routes_near, 1, near), (routes_far, near, n_own)):
+        for c in range(capacity):
+            for k in range(first, last):
+                routed[k, c] = pick(k, c)
+                to_own(k, routed.at[k, c], grad.at[c, own, me], group, c)
     for c in range(capacity):
-        for k in range(1, n_own):
-            routed[k, c] = pick(k, c)
-            group = routes_near if k < near else routes_far
-            to_own(k, routed.at[k, c], grad.at[c, own, me], group, c)
         grad[c, own, me] = pick(0, c)
 
     for copy in root_pieces[n_dp - 1 :]:
         send_root(*copy)
+    for copy in local[1:]:
+        copy.start()
 
     def half_of(c, far, at):
         start = near - base if far else base
@@ -250,20 +252,24 @@
             device_id_type=MESH,
         ).start()
 
+    def first_to(c, far):
+        return 1 + (c + far) % 2
+
     def spread_arrived(c, far, at):
         wait_for(spread_recv.at[c, far, at], half_of(c, far, at))
 
     def start_spread(c, far):
         arrived(routes_far if far else routes_near, c)
-        for k in (2, 1) if far else (1, 2):
-            spread(c, far, k, 0)
+        first = first_to(c, far)
+        spread(c, far, first, 0)
+        spread(c, far, 3 - first, 0)
 
     def relay(c, far):
-        came = 2 if far else 1
+        came = first_to(c, far)
         spread_arrived(c, far, came)
         spread(c, far, 3 - came, came)
 
-    halves = [(c, far) for c in range(capacity) for far in range(2)]
+    halves = [(c, far) for far in range(2) for c in range(capacity)]
     lag = 2
     for at, half in enumerate(halves):
         start_spread(*half)
@@ -303,7 +309,7 @@
 
     for c in range(capacity):
         for far in range(2):
-            spread_arrived(c, far, 1 if far else 2)
+            spread_arrived(c, far, 3 - first_to(c, far))
             spread_arrived(c, far, 3)
         half = jnp.concatenate(
             [
@@ -328,33 +334,31 @@
         for k in reversed(range(1, n_own)):
             to_own(k, sent_back.at[c, own_of[k]], came_back.at[c, own], backs, c)
         came_back[c, own] = sent_back[c, own]
-
-    for c in range(capacity):
         squares = jnp.square(grad[c].reshape(width, width).astype(jnp.float32))
         grad_sq = jnp.sum(squares.reshape(width // 8, 8, width), axis=0)
+        grad_all = jnp.sum(grad_sq, keepdims=True).reshape(1, 1)
         arrived(norms, c)
         prod_sq = norm_sent[c]
         for k in range(1, n_dp):
             prod_sq += norm_came[c, k]
         prod_all = jnp.sum(prod_sq, keepdims=True).reshape(1, 1)
-        grad_all = jnp.sum(grad_sq, keepdims=True).reshape(1, 1)
         ratio = jnp.sqrt(grad_all / cells) / jnp.sqrt(prod_all / cells + epsilon)
-        ratio_all[own, c] = jnp.broadcast_to(ratio, (8, LANES))
-    for k in range(1, n_own):
-        to_own(k, ratio_all.at[own], ratio_all.at[own], ratios, 0)
-    for c in range(capacity):
+        ratio_all[c, own] = jnp.broadcast_to(ratio, (8, LANES))
+        for k in reversed(range(1, n_own)):
+            to_own(k, ratio_all.at[c, own], ratio_all.at[c, own], ratios, c)
         statistics(c)
+
 
     for c in range(capacity):
         arrived(backs, c)
-    arrived(ratios)
+        arrived(ratios, c)
     for b in range(blocks):
-        ratio = ratio_all[named[b], slot_of[b]][0:1, :]
+        ratio = ratio_all[slot_of[b], named[b]][0:1, :]
         terms = came_back[slot_of[b], named[b]].astype(jnp.float32)
         update_ref[b] = (terms * ratio).astype(jnp.bfloat16)
 
     for group in sizes:
-        for c in range(1 if group in (sums, roots, ratios) else capacity):
+        for c in range(1 if group in (sums, roots) else capacity):
             wait_for(send_sem.at[group, c], sizes[group])
     for c, far in halves:
         for k in range(1, n_dp):
@@ -400,7 +404,7 @@
             pltpu.VMEM((capacity, n_own, strip, quarter), bf16),
             pltpu.VMEM((capacity, 8, LANES), f32),
             pltpu.VMEM((capacity, n_dp, 8, LANES), f32),
-            pltpu.VMEM((n_own, capacity, 8, LANES), f32),
+            pltpu.VMEM((capacity, n_own, 8, LANES), f32),
             dma((4 + n_dp,)),
             dma((7, capacity)),
             dma((7, capacity)),

time: 42.3 us -> 42.7 us (level)
  no operation moved by 1% of the time
where the time goes in v6:
time: 42.7 us; the launch traced here: 42.5 us
  Pallas kernels  41.9 us (98%)
  between operations  0.64 us (1%)
    pallas_call x1, Pallas kernels, fused(): pl.pallas_call(functools.partial(kernel, n_dp, n_own), out_shape=tuple((p...  40.9 us
    pallas_call x1, Pallas kernels, fused(): pl.pallas_call(write_out, out_shape=tuple((jax.ShapeDtypeStruct(shape, ki...  1.03 us

profile of v6, /device:TPU:0, one launch (start us, length us, event | category | flops | bytes accessed | tf_op | source)
XLA Modules:
  0.0 42.5 jit_solution(3252996598371813)
XLA Ops:
  0.6 40.9 %shard_map.85 = (f32[2,128,512]{2,1,0:T(8,128)S(1)}, f32[2,128,512]{2,1,0:T(8,128)S(1)}, bf16[8,64,128]{2,1,0:T(8,128)(2,1)S(1)}) custom-call(s32[8]{0:T(128)} %owner_ref.1, bf16[8,4,16,512]{3,2,1,0:T(8,128)(2,1)} %bitcast.1, f32[2,128,512]{2,1,0:T(8,128)} %left_stat_ref.1, f32[2,128,512]{2,1,0:T(8,128)} %right_stat_ref.1, ...), custom_call_target="tpu_custom_call" | custom-call | tf_op jit(solution)/shard_map/pallas_call | solution.py:389
  41.5 1.0 %shard_map.86 = (f32[2,128,512]{2,1,0:T(8,128)}, f32[2,128,512]{2,1,0:T(8,128)}, bf16[8,64,128]{2,1,0:T(8,128)(2,1)}) custom-call(f32[2,128,512]{2,1,0:T(8,128)S(1)} %get-tuple-element.6.refs_0_, f32[2,128,512]{2,1,0:T(8,128)S(1)} %get-tuple-element.7.refs_1_, bf16[8,64,128]{2,1,0:T(8,128)(2,1)S(1)} %get-tuple-element.8.refs_2_), custom_call_target="tpu_custom_call" | custom-call | tf_op jit(solution)/shard_map/pallas_call | solution.py:425

commit v7 on v6

--- a/solution.py
+++ b/solution.py
@@ -233,7 +233,7 @@
 
     for copy in root_pieces[n_dp - 1 :]:
         send_root(*copy)
-    for copy in local[1:]:
+    for copy in local[4:] + local[1:4]:
         copy.start()
 
     def half_of(c, far, at):
@@ -269,14 +269,10 @@
         spread_arrived(c, far, came)
         spread(c, far, 3 - came, came)
 
-    halves = [(c, far) for far in range(2) for c in range(capacity)]
-    lag = 2
-    for at, half in enumerate(halves):
-        start_spread(*half)
-        if at >= lag:
-            relay(*halves[at - lag])
-
-    for copy in local[1:]:
+    for c in range(capacity):
+        start_spread(c, 0)
+
+    for copy in local[4:] + local[1:2]:
         copy.wait()
     arrived(roots)
     for c in range(capacity):
@@ -284,8 +280,12 @@
             left_full[c, j, :, pl.ds(i * quarter, quarter)] = left_full[
                 c, i, :, pl.ds(j * quarter, quarter)
             ].T
-    for half in halves[-lag:]:
-        relay(*half)
+
+    for c in range(capacity):
+        start_spread(c, 1)
+        relay(c, 0)
+    for c in range(capacity):
+        relay(c, 1)
 
     cells = float(width * width)
     nt = (((1,), (1,)), ((), ()))
@@ -334,6 +334,8 @@
         for k in reversed(range(1, n_own)):
             to_own(k, sent_back.at[c, own_of[k]], came_back.at[c, own], backs, c)
         came_back[c, own] = sent_back[c, own]
+
+    for c in range(capacity):
         squares = jnp.square(grad[c].reshape(width, width).astype(jnp.float32))
         grad_sq = jnp.sum(squares.reshape(width // 8, 8, width), axis=0)
         grad_all = jnp.sum(grad_sq, keepdims=True).reshape(1, 1)
@@ -346,8 +348,10 @@
         ratio_all[c, own] = jnp.broadcast_to(ratio, (8, LANES))
         for k in reversed(range(1, n_own)):
             to_own(k, ratio_all.at[c, own], ratio_all.at[c, own], ratios, c)
+    local[2].wait()
+    local[3].wait()
+    for c in range(capacity):
         statistics(c)
-
 
     for c in range(capacity):
         arrived(backs, c)
@@ -360,9 +364,10 @@
     for group in sizes:
         for c in range(1 if group in (sums, roots) else capacity):
             wait_for(send_sem.at[group, c], sizes[group])
-    for c, far in halves:
-        for k in range(1, n_dp):
-            wait_for(spread_send.at[c, far, k], half_of(c, far, 0))
+    for c in range(capacity):
+        for far in range(2):
+            for k in range(1, n_dp):
+                wait_for(spread_send.at[c, far, k], half_of(c, far, 0))
 
 
 def write_out(*refs):

time: 42.7 us -> 40.4 us (0.946)
  Pallas kernels: 41.9 us -> 39.6 us
    pallas_call x1, Pallas kernels: 40.9 us -> 38.6 us  [fused(): pl.pallas_call(functools.partial(kernel, n_dp, n_own), out_shape=tuple((p...]
where the time goes in v7:
time: 40.4 us; the launch traced here: 40.2 us
  Pallas kernels  39.6 us (98%)
  between operations  0.64 us (2%)
    pallas_call x1, Pallas kernels, fused(): pl.pallas_call(functools.partial(kernel, n_dp, n_own), out_shape=tuple((p...  38.6 us
    pallas_call x1, Pallas kernels, fused(): pl.pallas_call(write_out, out_shape=tuple((jax.ShapeDtypeStruct(shape, ki...  1.03 us

profile of v7, /device:TPU:0, one launch (start us, length us, event | category | flops | bytes accessed | tf_op | source)
XLA Modules:
  0.0 40.2 jit_solution(17775951214556910800)
XLA Ops:
  0.6 38.6 %shard_map.85 = (f32[2,128,512]{2,1,0:T(8,128)S(1)}, f32[2,128,512]{2,1,0:T(8,128)S(1)}, bf16[8,64,128]{2,1,0:T(8,128)(2,1)S(1)}) custom-call(s32[8]{0:T(128)} %owner_ref.1, bf16[8,4,16,512]{3,2,1,0:T(8,128)(2,1)} %bitcast.1, f32[2,128,512]{2,1,0:T(8,128)} %left_stat_ref.1, f32[2,128,512]{2,1,0:T(8,128)} %right_stat_ref.1, ...), custom_call_target="tpu_custom_call" | custom-call | tf_op jit(solution)/shard_map/pallas_call | solution.py:394
  39.2 1.0 %shard_map.86 = (f32[2,128,512]{2,1,0:T(8,128)}, f32[2,128,512]{2,1,0:T(8,128)}, bf16[8,64,128]{2,1,0:T(8,128)(2,1)}) custom-call(f32[2,128,512]{2,1,0:T(8,128)S(1)} %get-tuple-element.6.refs_0_, f32[2,128,512]{2,1,0:T(8,128)S(1)} %get-tuple-element.7.refs_1_, bf16[8,64,128]{2,1,0:T(8,128)(2,1)S(1)} %get-tuple-element.8.refs_2_), custom_call_target="tpu_custom_call" | custom-call | tf_op jit(solution)/shard_map/pallas_call | solution.py:430

commit v8 on v7

--- a/solution.py
+++ b/solution.py
@@ -138,9 +138,13 @@
         pltpu.make_async_copy(like, like, sem).wait()
 
     sums, roots, routes_near, routes_far, norms, backs, ratios = range(7)
+    roots_x, roots_y, roots_across = range(7, 10)
     sizes = {
         sums: parts.at[pl.ds(1, n_dp - 1)],
-        roots: left_full.at[:, pl.ds(1, n_dp - 1), :, pl.ds(0, 2 * quarter)],
+        roots: left_full.at[:, pl.ds(1, n_dp - 1), :, pl.ds(0, quarter)],
+        roots_x: left_full.at[:, 1, :, pl.ds(0, quarter)],
+        roots_y: left_full.at[:, 2, :, pl.ds(0, quarter)],
+        roots_across: left_full.at[:, 3, :, pl.ds(0, quarter)],
         routes_near: grad.at[0, pl.ds(1, near - 1), 0],
         routes_far: grad.at[0, pl.ds(0, near), 0],
         norms: norm_came.at[0, pl.ds(1, n_dp - 1)],
@@ -178,20 +182,21 @@
     for k in reversed(range(1, n_dp)):
         to_dp(k, grads_ref.at[:, dp_of[k]], parts.at[k], sums, 0)
 
-    def send_root(k, column, slots):
+    def send_root(k, column, slots, group):
         columns = pl.ds(pl.multiple_of(dp_of[k ^ column] * quarter, LANES), quarter)
         to_dp(
             k,
             left_root_ref.at[slots, :, columns],
             left_full.at[slots, k, :, pl.ds(column * quarter, quarter)],
-            roots,
+            group,
             0,
         )
 
     every = pl.ds(0, capacity)
-    root_pieces = [(1, 1, every), (2, 2, every), (3, 3, every), (1, 3, every), (2, 3, every)]
-    root_pieces += [(1 + c % 2, 2 - c % 2, pl.ds(c, 1)) for c in range(capacity)]
-    for copy in root_pieces[: n_dp - 1]:
+    root_pieces = [(1, 1, every, roots_x), (2, 2, every, roots_y)]
+    root_pieces += [(1, 3, every, roots), (2, 3, every, roots)]
+    root_pieces += [(1 + c % 2, 2 - c % 2, pl.ds(c, 1), roots) for c in range(capacity)]
+    for copy in root_pieces[:3]:
         send_root(*copy)
 
     named = [owner_ref[b] for b in range(blocks)]
@@ -231,7 +236,7 @@
     for c in range(capacity):
         grad[c, own, me] = pick(0, c)
 
-    for copy in root_pieces[n_dp - 1 :]:
+    for copy in root_pieces[3:]:
         send_root(*copy)
     for copy in local[4:] + local[1:4]:
         copy.start()
@@ -269,7 +274,19 @@
         spread_arrived(c, far, came)
         spread(c, far, 3 - came, came)
 
-    for c in range(capacity):
+    start_spread(0, 0)
+    arrived(roots_x)
+    arrived(roots_y)
+    for c in range(capacity):
+        came = 1 + c % 2
+        to_dp(
+            3 - came,
+            left_full.at[c, came, :, pl.ds(came * quarter, quarter)],
+            left_full.at[c, 3, :, pl.ds(3 * quarter, quarter)],
+            roots_across,
+            0,
+        )
+    for c in range(1, capacity):
         start_spread(c, 0)
 
     for copy in local[4:] + local[1:2]:
@@ -307,6 +324,7 @@
         right_gram = lax.dot_general(mine, whole, tn, preferred_element_type=jnp.float32)
         new_right_ref[c] = decay * right_old[c] + right_gram * (1.0 / width)
 
+    arrived(roots_across)
     for c in range(capacity):
         for far in range(2):
             spread_arrived(c, far, 3 - first_to(c, far))
@@ -362,7 +380,7 @@
         update_ref[b] = (terms * ratio).astype(jnp.bfloat16)
 
     for group in sizes:
-        for c in range(1 if group in (sums, roots) else capacity):
+        for c in range(capacity if group in (routes_near, routes_far, norms, backs, ratios) else 1):
             wait_for(send_sem.at[group, c], sizes[group])
     for c in range(capacity):
         for far in range(2):
@@ -372,9 +390,19 @@
 
 def write_out(*refs):
     inputs, outputs, sems = refs[:3], refs[3:6], refs[6]
-    copies = [
-        pltpu.make_async_copy(inputs[i], outputs[i], sems.at[i]) for i in range(len(inputs))
-    ]
+    copies = []
+    for i, parts in enumerate((4, 4, 2)):
+        size = inputs[i].shape[0] * inputs[i].shape[1] // parts
+        step = min(size, inputs[i].shape[1])
+        deep = size // step
+        for part in range(parts):
+            first, row = divmod(part * size, inputs[i].shape[1])
+            piece = (pl.ds(first, deep), pl.ds(row, step))
+            copies.append(
+                pltpu.make_async_copy(
+                    inputs[i].at[piece], outputs[i].at[piece], sems.at[len(copies)]
+                )
+            )
     for copy in copies:
         copy.start()
     for copy in copies:
@@ -411,8 +439,8 @@
             pltpu.VMEM((capacity, n_dp, 8, LANES), f32),
             pltpu.VMEM((capacity, n_own, 8, LANES), f32),
             dma((4 + n_dp,)),
-            dma((7, capacity)),
-            dma((7, capacity)),
+            dma((10, capacity)),
+            dma((10, capacity)),
             dma((capacity, 2, n_dp)),
             dma((capacity, 2, n_dp)),
         ],
@@ -432,7 +460,7 @@
         out_shape=tuple(jax.ShapeDtypeStruct(shape, kind) for shape, kind in zip(shapes, types)),
         in_specs=[anywhere] * 3,
         out_specs=tuple([pl.BlockSpec(memory_space=pltpu.HBM)] * 3),
-        scratch_shapes=[dma((3,))],
+        scratch_shapes=[dma((10,))],
         compiler_params=pltpu.CompilerParams(vmem_limit_bytes=4 * 1024 * 1024),
     )(*[pltpu.with_memory_space_constraint(x, pltpu.VMEM) for x in results])
 

time: 40.4 us -> 41.1 us (1.017)
  Pallas kernels: 39.6 us -> 40.3 us
    pallas_call x1, Pallas kernels: 38.6 us -> 39.3 us  [fused(): pl.pallas_call(functools.partial(kernel, n_dp, n_own), out_shape=tuple((p...]
where the time goes in v8:
time: 41.1 us; the launch traced here: 41 us
  Pallas kernels  40.3 us (98%)
  between operations  0.64 us (2%)
    pallas_call x1, Pallas kernels, fused(): pl.pallas_call(functools.partial(kernel, n_dp, n_own), out_shape=tuple((p...  39.3 us
    pallas_call x1, Pallas kernels, fused(): pl.pallas_call(write_out, out_shape=tuple((jax.ShapeDtypeStruct(shape, ki...  1.08 us

profile of v8, /device:TPU:0, one launch (start us, length us, event | category | flops | bytes accessed | tf_op | source)
XLA Modules:
  0.0 41.0 jit_solution(7917020747945944709)
XLA Ops:
  0.6 39.3 %shard_map.85 = (f32[2,128,512]{2,1,0:T(8,128)S(1)}, f32[2,128,512]{2,1,0:T(8,128)S(1)}, bf16[8,64,128]{2,1,0:T(8,128)(2,1)S(1)}) custom-call(s32[8]{0:T(128)} %owner_ref.1, bf16[8,4,16,512]{3,2,1,0:T(8,128)(2,1)} %bitcast.1, f32[2,128,512]{2,1,0:T(8,128)} %left_stat_ref.1, f32[2,128,512]{2,1,0:T(8,128)} %right_stat_ref.1, ...), custom_call_target="tpu_custom_call" | custom-call | tf_op jit(solution)/shard_map/pallas_call | solution.py:422
  39.9 1.1 %shard_map.86 = (f32[2,128,512]{2,1,0:T(8,128)}, f32[2,128,512]{2,1,0:T(8,128)}, bf16[8,64,128]{2,1,0:T(8,128)(2,1)}) custom-call(f32[2,128,512]{2,1,0:T(8,128)S(1)} %get-tuple-element.6.refs_0_, f32[2,128,512]{2,1,0:T(8,128)S(1)} %get-tuple-element.7.refs_1_, bf16[8,64,128]{2,1,0:T(8,128)(2,1)S(1)} %get-tuple-element.8.refs_2_), custom_call_target="tpu_custom_call" | custom-call | tf_op jit(solution)/shard_map/pallas_call | solution.py:458

commit v9 on v7

--- a/solution.py
+++ b/solution.py
@@ -100,6 +100,7 @@
     norm_sent,
     norm_came,
     ratio_all,
+    half_rows,
     local_sem,
     send_sem,
     recv_sem,
@@ -169,10 +170,10 @@
     local[0].start()
 
     barrier = pltpu.get_barrier_semaphore()
-    for k in range(1, n_dp):
+    for k in reversed(range(1, n_own)):
+        pl.semaphore_signal(barrier, inc=1, device_id=(me, own_of[k]), device_id_type=MESH)
+    for k in reversed(range(1, n_dp)):
         pl.semaphore_signal(barrier, inc=1, device_id=(dp_of[k], own), device_id_type=MESH)
-    for k in range(1, n_own):
-        pl.semaphore_signal(barrier, inc=1, device_id=(me, own_of[k]), device_id_type=MESH)
     pl.semaphore_wait(barrier, n_dp - 1 + n_own - 1)
 
     for k in reversed(range(1, n_dp)):
@@ -311,15 +312,16 @@
         for far in range(2):
             spread_arrived(c, far, 3 - first_to(c, far))
             spread_arrived(c, far, 3)
-        half = jnp.concatenate(
-            [
-                lax.dot_general(
-                    grad_rows(c, k), right_quarter[c], nt, preferred_element_type=jnp.float32
+            first = (near - base if far else base) // per_quarter
+            for i in range(near // per_quarter):
+                piece = grad[c, pl.ds((first + i) * per_quarter, per_quarter)]
+                half_rows[c, first + i] = lax.dot_general(
+                    piece.reshape(quarter, width),
+                    right_quarter[c],
+                    nt,
+                    preferred_element_type=jnp.float32,
                 ).astype(jnp.bfloat16)
-                for k in range(n_dp)
-            ],
-            axis=0,
-        )
+        half = jnp.concatenate([half_rows[c, dp_of[k]] for k in range(n_dp)], axis=0)
         product = jnp.dot(
             left_full[c].reshape(width, width), half, preferred_element_type=jnp.float32
         )
@@ -410,6 +412,7 @@
             pltpu.VMEM((capacity, 8, LANES), f32),
             pltpu.VMEM((capacity, n_dp, 8, LANES), f32),
             pltpu.VMEM((capacity, n_own, 8, LANES), f32),
+            pltpu.VMEM((capacity, n_dp, quarter, quarter), bf16),
             dma((4 + n_dp,)),
             dma((7, capacity)),
             dma((7, capacity)),

time: 40.4 us -> 40.6 us (level)
  no operation moved by 1% of the time
where the time goes in v9:
time: 40.6 us; the launch traced here: 40.4 us
  Pallas kernels  39.8 us (98%)
  between operations  0.64 us (2%)
    pallas_call x1, Pallas kernels, fused(): pl.pallas_call(functools.partial(kernel, n_dp, n_own), out_shape=tuple((p...  38.7 us
    pallas_call x1, Pallas kernels, fused(): pl.pallas_call(write_out, out_shape=tuple((jax.ShapeDtypeStruct(shape, ki...  1.03 us

profile of v9, /device:TPU:0, one launch (start us, length us, event | category | flops | bytes accessed | tf_op | source)
XLA Modules:
  0.0 40.4 jit_solution(10509923741923959779)
XLA Ops:
  0.6 38.7 %shard_map.85 = (f32[2,128,512]{2,1,0:T(8,128)S(1)}, f32[2,128,512]{2,1,0:T(8,128)S(1)}, bf16[8,64,128]{2,1,0:T(8,128)(2,1)S(1)}) custom-call(s32[8]{0:T(128)} %owner_ref.1, bf16[8,4,16,512]{3,2,1,0:T(8,128)(2,1)} %bitcast.1, f32[2,128,512]{2,1,0:T(8,128)} %left_stat_ref.1, f32[2,128,512]{2,1,0:T(8,128)} %right_stat_ref.1, ...), custom_call_target="tpu_custom_call" | custom-call | tf_op jit(solution)/shard_map/pallas_call | solution.py:396
  39.4 1.0 %shard_map.86 = (f32[2,128,512]{2,1,0:T(8,128)}, f32[2,128,512]{2,1,0:T(8,128)}, bf16[8,64,128]{2,1,0:T(8,128)(2,1)}) custom-call(f32[2,128,512]{2,1,0:T(8,128)S(1)} %get-tuple-element.6.refs_0_, f32[2,128,512]{2,1,0:T(8,128)S(1)} %get-tuple-element.7.refs_1_, bf16[8,64,128]{2,1,0:T(8,128)(2,1)S(1)} %get-tuple-element.8.refs_2_), custom_call_target="tpu_custom_call" | custom-call | tf_op jit(solution)/shard_map/pallas_call | solution.py:433
